TPU v7x, 32 devices: a whole 2x2x4 slice. The times are simulated.
32 devices in a mesh: chain: 2 (over y), cell: 4 (over z), col: 4 (over x, core).
Axes of the slice: x: 2, y: 2, z: 4, core: 2. Of those that a mesh axis runs over, the one named last changes fastest.
Arguments:
- grad: float32 [16384, 64], P(('chain', 'cell', 'col')), parts along dimension 0, may hold values from -6 to 6
- near_tiles: bfloat16 [4, 2, 2048, 2048], P('cell', None, 'col'), may hold values from -0.09375 to 0.09375
- tile_count: int32 [4], replicated, may hold values from 1 to 2
- near_offset: int32 [4], replicated, may hold values from -2 to 2, as said below
- far_src: int32 [4, 8], replicated, may hold values from 0 to 3
- far_count: int32 [4], replicated, may hold values from 1 to 8
- far_cores: float32 [4, 8, 64, 64], P('cell'), may hold values from -0.25 to 0.25
- basis_out: bfloat16 [8192, 64], P(('cell', 'col')), may hold values from -0.75 to 0.75
- basis_in: bfloat16 [8192, 64], P(('cell', 'col')), may hold values from -0.125 to 0.125
Outputs:
- step_block: float32 [16384, 64], P(('chain', 'cell', 'col')), parts along dimension 0
There are 2 independent parts, one for each index of `chain`. A program takes and returns all parts, laid end to end along the dimension named above; an argument that names none is the same for every part. Nothing has to cross between parts.
Inputs may be any that keep to these rules, and one draw needn't show every extreme that they name: c + near_offset[c] is a cluster of the chain, and near_offset[c] is never 0.
All inputs are finite; a program needn't handle non-finite values.
Results may differ from a plain program's by a relative error of at most 0.0035.
Values may be sent and summed in bfloat16 or wider, within the bound.
A program may use at most 64 MiB of HBM per device.

v0:
```python
import jax
import jax.numpy as jnp
from jax import lax
from jax.sharding import PartitionSpec as P


def shifted(value, axis, by):
    devices = lax.axis_size(axis)
    pairs = [(i, i + by) for i in range(devices) if 0 <= i + by < devices]
    return lax.ppermute(value, axis, pairs)


def pick_offset(stacked, offset):
    position = offset + 2 - (offset > 0).astype(jnp.int32)
    return lax.dynamic_index_in_dim(stacked, position, 0, keepdims=False)


def coupling(table, sources, count, cores):
    picked = jnp.take(table, sources, axis=0)
    slots = jnp.arange(cores.shape[0], dtype=jnp.int32)
    masked = jnp.where((slots < count)[:, None, None], cores, jnp.zeros_like(cores))
    return jnp.einsum("kab,kbw->aw", masked, picked, precision=lax.Precision.HIGHEST)


def body(
    grad, near_tiles, tile_count, near_offset, far_src, far_count, far_cores, basis_out, basis_in
):
    owner = lax.axis_index("cell")
    rounded = grad.astype(jnp.bfloat16)
    offset = near_offset[owner]
    steps_list = (-2, -1, 1, 2)
    whole = lax.all_gather(rounded, "col", axis=0, tiled=True)
    moved = [shifted(whole, "cell", -step) for step in steps_list]
    beside = pick_offset(jnp.stack(moved), offset)
    tiles = near_tiles[0]
    own_term = jnp.dot(tiles[0], whole, preferred_element_type=jnp.float32)
    other_term = jnp.dot(tiles[1], beside, preferred_element_type=jnp.float32)
    near = own_term + jnp.where(tile_count[owner] == 2, other_term, jnp.zeros_like(other_term))
    partial_proj = lax.dot_general(
        basis_in, rounded, (((0,), (0,)), ((), ())), preferred_element_type=jnp.float32
    )
    sources = far_src[owner]
    count = far_count[owner]
    cores = far_cores[0]
    proj = lax.psum(partial_proj, "col")
    table = lax.all_gather(proj[None], "cell", axis=0, tiled=True)
    core_block = coupling(table, sources, count, cores).astype(jnp.bfloat16)
    far = jnp.dot(basis_out, core_block, preferred_element_type=jnp.float32)
    return near + far


def solution(mesh):
    placed = (
        P(("chain", "cell", "col"), None),
        P("cell", None, "col", None),
        P(),
        P(),
        P(),
        P(),
        P("cell", None, None, None),
        P(("cell", "col"), None),
        P(("cell", "col"), None),
    )
    return jax.shard_map(
        body,
        mesh=mesh,
        in_specs=placed,
        out_specs=P(("chain", "cell", "col"), None),
        check_vma=False,
    )
```

profile of v0, /device:TPU:0, one launch (start us, length us, event | category | flops | bytes accessed | tf_op | source)
XLA Modules:
  0.0 60.8 jit_solution(2780922674257491303)
XLA Ops:
  0.0 0.0 copy-start
  0.0 0.9 %convert_element_type.10 = bf16[512,64]{0,1:T(8,128)(2,1)S(1)} convert(f32[512,64]{0,1:T(8,128)} %param.9) | non-fusion elementwise | flops 32768 | bytes 196608 | tf_op jit(solution)/shard_map/convert_element_type | solution.py:29
  1.0 7.2 %all_gather.6 = bf16[2048,64]{0,1:T(8,128)(2,1)S(1)} all-gather(bf16[512,64]{0,1:T(8,128)(2,1)S(1)} %convert_element_type.10), channel_id=1, replica_groups=mesh['chain'=2,'cell'=4,'col'=4] {'col'}, dimensions={0}, use_global_device_ids=true | all-gather | bytes 327680 | tf_op jit(solution)/shard_map/all_gather | solution.py:32
  8.1 4.5 %collective-permute-start = (bf16[2048,64]{0,1:T(8,128)(2,1)S(1)}, bf16[2048,64]{0,1:T(8,128)(2,1)S(1)}, u32[]{:S(2)}, u32[]{:S(2)}) collective-permute-start(bf16[2048,64]{0,1:T(8,128)(2,1)S(1)} %all_gather.6), channel_id=1, source_target_pairs={{0,8},{4,12},{1,9},{5,13},{2,10},{6,14},{3,11},{7,15},{16,24},{20,... | collective-permute-start | bytes 786440 | tf_op jit(solution)/shard_map/ppermute | solution.py:10
  12.7 3.5 %collective-permute-start.1 = (bf16[2048,64]{0,1:T(8,128)(2,1)S(1)}, bf16[2048,64]{0,1:T(8,128)(2,1)S(1)}, u32[]{:S(2)}, u32[]{:S(2)}) collective-permute-start(bf16[2048,64]{0,1:T(8,128)(2,1)S(1)} %all_gather.6), channel_id=1, source_target_pairs={{0,4},{4,8},{8,12},{1,5},{5,9},{9,13},{2,6},{6,10},{10,14},{3,7},{... | collective-permute-start | bytes 786440 | tf_op jit(solution)/shard_map/ppermute | solution.py:10
  16.2 1.3 %collective-permute-start.2 = (bf16[2048,64]{0,1:T(8,128)(2,1)S(1)}, bf16[2048,64]{0,1:T(8,128)(2,1)S(1)}, u32[]{:S(2)}, u32[]{:S(2)}) collective-permute-start(bf16[2048,64]{0,1:T(8,128)(2,1)S(1)} %all_gather.6), channel_id=1, source_target_pairs={{4,0},{8,4},{12,8},{5,1},{9,5},{13,9},{6,2},{10,6},{14,10},{7,3},{... | collective-permute-start | bytes 786440 | tf_op jit(solution)/shard_map/ppermute | solution.py:10
  17.5 1.3 %collective-permute-start.3 = (bf16[2048,64]{0,1:T(8,128)(2,1)S(1)}, bf16[2048,64]{0,1:T(8,128)(2,1)S(1)}, u32[]{:S(2)}, u32[]{:S(2)}) collective-permute-start(bf16[2048,64]{0,1:T(8,128)(2,1)S(1)} %all_gather.6), channel_id=1, source_target_pairs={{8,0},{12,4},{9,1},{13,5},{10,2},{14,6},{11,3},{15,7},{24,16},{28,... | collective-permute-start | bytes 786440 | tf_op jit(solution)/shard_map/ppermute | solution.py:10
  18.8 1.2 %dynamic_slice.19 = s32[1]{0:T(128)} dynamic-slice(s32[4]{0:T(128)} %param.14, s32[]{:T(128)S(6)} %select_n.45), dynamic_slice_sizes={1} | dynamic-slice | bytes 12 | tf_op jit(solution)/shard_map/dynamic_slice | solution.py:43
  20.0 0.7 %fusion.30 = s32[8]{0:T(128)S(1)} fusion(s32[4,8]{1,0:T(4,128)} %param.13, s32[]{:T(128)S(6)} %select_n.45), kind=kLoop, calls=%fused_computation.35 | loop fusion | flops 24 | bytes 68 | tf_op jit(solution)/shard_map/jit(_take)/jit(_where)/select_n | solution.py:19
  20.7 1.3 %compare_and_fusion = (pred[8]{0:T(512)(128)(4,1)S(1)}, pred[8]{0:T(512)(128)(4,1)S(1)}) fusion(s32[4,8]{1,0:T(4,128)} %param.13, s32[]{:T(128)S(6)} %select_n.45, s32[]{:T(128)} %bitcast.10), kind=kLoop, calls=%fused_computation.32 | loop fusion | flops 56 | bytes 56 | tf_op jit(solution)/shard_map/jit(_take)/and | solution.py:19
  22.1 1.0 %convolution_bitcast_fusion.1 = f32[1,64,64]{2,1,0:T(8,128)S(1)} fusion(bf16[512,64]{0,1:T(8,128)(2,1)} %param.17, bf16[512,64]{0,1:T(8,128)(2,1)S(1)} %convert_element_type.10), kind=kOutput, calls=%fused_computation.12 | convolution fusion | flops 4194304 | bytes 147456 | tf_op jit(solution)/shard_map/dot_general | solution.py:39
  23.1 11.4 %psum.7 = f32[1,64,64]{2,1,0:T(8,128)S(1)} all-reduce(f32[1,64,64]{2,1,0:T(8,128)S(1)} %convolution_bitcast_fusion.1), channel_id=1, replica_groups=mesh['chain'=2,'cell'=4,'col'=4] {'col'}, use_global_device_ids=true, to_apply=%region_0.1 | all-reduce | flops 4096 | bytes 32768 | tf_op jit(solution)/shard_map/psum | solution.py:45
  34.5 14.3 %all_gather.7 = f32[4,64,64]{2,1,0:T(8,128)S(1)} all-gather(f32[1,64,64]{2,1,0:T(8,128)S(1)} %psum.7), channel_id=1, replica_groups=mesh['chain'=2,'cell'=4,'col'=4] {'cell'}, dimensions={0}, use_global_device_ids=true | all-gather | bytes 81920 | tf_op jit(solution)/shard_map/all_gather | solution.py:46
  48.7 0.6 gather_fusion
  49.3 1.4 %fusion.18 = bf16[64,64]{1,0:T(8,128)(2,1)S(1)} fusion(f32[1,8,64,64]{3,2,1,0:T(8,128)} %param.15, f32[8,64,64]{2,1,0:T(8,128)S(1)} %gather_fusion, pred[8]{0:T(512)(128)(4,1)S(1)} %get-tuple-element.5, pred[8]{0:T(512)(128)(4,1)S(1)} %get-tuple-element.6), kind=kOutput, calls=%fused_computation.14 | convolution fusion | flops 25235456 | bytes 270352 | tf_op jit(solution)/shard_map/kab,kbw->aw/dot_general | solution.py:22
  50.7 1.2 %dynamic_slice.17 = s32[1]{0:T(128)} dynamic-slice(s32[4]{0:T(128)} %param.12, s32[]{:T(128)S(6)} %select_n.45), dynamic_slice_sizes={1} | dynamic-slice | bytes 12 | tf_op jit(solution)/shard_map/dynamic_slice | solution.py:30
  53.3 1.3 %dynamic_slice.16 = s32[1]{0:T(128)} dynamic-slice(s32[4]{0:T(128)} %param.11, s32[]{:T(128)S(6)} %select_n.45), dynamic_slice_sizes={1} | dynamic-slice | bytes 12 | tf_op jit(solution)/shard_map/dynamic_slice | solution.py:38
  55.2 0.0 copy-done
  55.2 0.2 convolution_bitcast_fusion
  55.4 0.0 collective-permute-done
  55.4 0.0 collective-permute-done.1
  55.4 0.0 collective-permute-done.2
  55.4 0.0 collective-permute-done.3
  55.4 2.4 %fusion.15 = f32[512,64]{0,1:T(8,128)S(1)} fusion(bf16[1,2,512,2048]{3,2,1,0:T(8,128)(2,1)} %param.10, s32[]{:T(128)S(6)} %select_n.47, bf16[1,2048,64]{1,2,0:T(8,128)(2,1)S(1)} %bitcast.48, bf16[1,2048,64]{1,2,0:T(8,128)(2,1)S(1)} %bitcast.49, bf16[1,2048,64]{1,2,0:T(8,128)(2,1)S(1)} %bitcast.50, bf16[1,2048,64]{1,2,0:T(8,128)(2,1)S(1)} %bitcast.51, ...), kind=kOutput, calls=%fused_computation.10 | convolution fusion | flops 134643712 | bytes 3277316 | tf_op jit(solution)/shard_map/dot_general | solution.py:37
  57.8 3.0 %fusion.9 = f32[512,64]{0,1:T(8,128)} fusion(f32[512,64]{0,1:T(8,128)S(1)} %convolution_bitcast_fusion, f32[512,64]{0,1:T(8,128)S(1)} %fusion.15, bf16[2048,64]{0,1:T(8,128)(2,1)S(1)} %all_gather.6, bf16[1,2,512,2048]{3,2,1,0:T(8,128)(2,1)} %param.10), kind=kOutput, calls=%fused_computation.8 | convolution fusion | flops 134283264 | bytes 2752512 | tf_op jit(solution)/shard_map/dot_general | solution.py:36
  (1 shorter events, 0.0 us)
Async XLA Ops:
  0.0 55.2 %copy-start = (bf16[512,64]{0,1:T(8,128)(2,1)S(1)}, bf16[512,64]{0,1:T(8,128)(2,1)}, u32[]{:S(2)}) copy-start(bf16[512,64]{0,1:T(8,128)(2,1)} %param.16) | copy-start | bytes 196612
  8.1 47.2 %collective-permute-start = (bf16[2048,64]{0,1:T(8,128)(2,1)S(1)}, bf16[2048,64]{0,1:T(8,128)(2,1)S(1)}, u32[]{:S(2)}, u32[]{:S(2)}) collective-permute-start(bf16[2048,64]{0,1:T(8,128)(2,1)S(1)} %all_gather.6), channel_id=1, source_target_pairs={{0,8},{4,12},{1,9},{5,13},{2,10},{6,14},{3,11},{7,15},{16,24},{20,... | collective-permute-start | bytes 786440 | tf_op jit(solution)/shard_map/ppermute | solution.py:10
  12.7 42.7 %collective-permute-start.1 = (bf16[2048,64]{0,1:T(8,128)(2,1)S(1)}, bf16[2048,64]{0,1:T(8,128)(2,1)S(1)}, u32[]{:S(2)}, u32[]{:S(2)}) collective-permute-start(bf16[2048,64]{0,1:T(8,128)(2,1)S(1)} %all_gather.6), channel_id=1, source_target_pairs={{0,4},{4,8},{8,12},{1,5},{5,9},{9,13},{2,6},{6,10},{10,14},{3,7},{... | collective-permute-start | bytes 786440 | tf_op jit(solution)/shard_map/ppermute | solution.py:10
  16.2 39.2 %collective-permute-start.2 = (bf16[2048,64]{0,1:T(8,128)(2,1)S(1)}, bf16[2048,64]{0,1:T(8,128)(2,1)S(1)}, u32[]{:S(2)}, u32[]{:S(2)}) collective-permute-start(bf16[2048,64]{0,1:T(8,128)(2,1)S(1)} %all_gather.6), channel_id=1, source_target_pairs={{4,0},{8,4},{12,8},{5,1},{9,5},{13,9},{6,2},{10,6},{14,10},{7,3},{... | collective-permute-start | bytes 786440 | tf_op jit(solution)/shard_map/ppermute | solution.py:10
  17.5 37.9 %collective-permute-start.3 = (bf16[2048,64]{0,1:T(8,128)(2,1)S(1)}, bf16[2048,64]{0,1:T(8,128)(2,1)S(1)}, u32[]{:S(2)}, u32[]{:S(2)}) collective-permute-start(bf16[2048,64]{0,1:T(8,128)(2,1)S(1)} %all_gather.6), channel_id=1, source_target_pairs={{8,0},{12,4},{9,1},{13,5},{10,2},{14,6},{11,3},{15,7},{24,16},{28,... | collective-permute-start | bytes 786440 | tf_op jit(solution)/shard_map/ppermute | solution.py:10
where the time goes:
time: 61.3 us; the launch traced here: 60.8 us
  blocking collectives  32.9 us (54%)
  starting transfers between devices  10.6 us (17%)
  matrix products  7.95 us (13%)
  local copies, waits for them, and re-layouts  4.33 us (7%)
  other arithmetic  2.98 us (5%)
  between operations  2.04 us (3%)
    all_gather x1, blocking collectives, body(): table = lax.all_gather(proj[None], 'cell', axis=0, tiled=True)  14.3 us
    psum x1, blocking collectives, body(): proj = lax.psum(partial_proj, 'col')  11.4 us
    ppermute x4, starting transfers between devices, shifted(): return lax.ppermute(value, axis, pairs)  10.6 us
    all_gather x1, blocking collectives, body(): whole = lax.all_gather(rounded, 'col', axis=0, tiled=True)  7.19 us
    dot_general x1, matrix products, body(): own_term = jnp.dot(tiles[0], whole, preferred_element_type=jnp.float32)  3.02 us
    dot_general x1, matrix products, body(): other_term = jnp.dot(tiles[1], beside, preferred_element_type=jnp.float32)  2.36 us
    dot_general x1, matrix products, coupling(): jnp.einsum('kab,kbw->aw', masked, picked, precision=lax.Precision.HIGHEST)  1.42 us
    and x1, other arithmetic, coupling(): picked = jnp.take(table, sources, axis=0)  1.34 us
  transfers between devices with their start and end apart: 4, of which 0 were waited for; matrix products, arithmetic and copies ran while one was open for 15% of the time, Pallas kernels for 0%

commit v1 on v0

v1 whole, which is shorter than its diff:
```python
import functools

import jax
import jax.numpy as jnp
from jax import lax
from jax.experimental import pallas as pl
from jax.experimental.pallas import tpu as pltpu
from jax.sharding import PartitionSpec as P

MESH = pl.DeviceIdType.MESH
OFFSETS = (-2, -1, 1, 2)
F32 = jnp.float32
BF16 = jnp.bfloat16


def remote(src, dst, send, recv, **where):
    return pltpu.make_async_remote_copy(
        src_ref=src, dst_ref=dst, send_sem=send, recv_sem=recv, device_id=where, device_id_type=MESH
    )


def kernel(
    n_cell, n_col,
    count_ref, offset_ref, fsrc_ref, fcount_ref, grad_hbm, tiles_hbm, cores_hbm, bout_hbm, bin_hbm,
    out_ref,
    grad, tiles, cores, bout, bin_,
    own, near, beside, ppt, part, table, coret, acc,
    local_sem, own_send, own_recv, near_send, near_recv, side_send, side_recv,
    part_send, part_recv, table_send, table_recv, core_send, core_recv,
):
    cell = lax.axis_index("cell")
    col = lax.axis_index("col")
    rows = grad.shape[0]
    half = rows // 2
    width = grad.shape[1]
    piece = width // n_col
    bits = [1 << b for b in reversed(range(n_col.bit_length() - 1))]

    def flip(d):
        value = col
        for b in bits:
            if d & b:
                value = value + b - 2 * b * lax.rem(value // b, 2)
        return value

    barrier = pltpu.get_barrier_semaphore()
    for d in range(1, n_col):
        pl.semaphore_signal(barrier, inc=1, device_id={"col": flip(d)}, device_id_type=MESH)
    for d in range(1, n_cell):
        pl.semaphore_signal(
            barrier, inc=1, device_id={"cell": lax.rem(cell + d, n_cell)}, device_id_type=MESH
        )

    loads = [
        pltpu.make_async_copy(src, dst, local_sem.at[i])
        for i, (src, dst) in enumerate((
            (grad_hbm, grad), (bin_hbm, bin_), (tiles_hbm.at[0, 0], tiles.at[0]),
            (cores_hbm.at[0], cores), (bout_hbm, bout), (tiles_hbm.at[0, 1], tiles.at[1]),
        ))
    ]
    for load in loads:
        load.start()

    loads[0].wait()
    rounded = grad[...].astype(BF16)
    own[col] = jnp.concatenate([rounded[:half], rounded[half:]], axis=1)
    loads[1].wait()
    ppt[...] = lax.dot_general(rounded, bin_[...], (((0,), (0,)), ((), ())), preferred_element_type=F32)
    for p, step in enumerate(OFFSETS):
        @pl.when((cell + step < 0) | (cell + step >= n_cell))
        def _():
            near[p] = jnp.zeros(near.shape[1:], BF16)

    pl.semaphore_wait(barrier, (n_col - 1) + (n_cell - 1))

    part_copies = [
        remote(ppt.at[pl.ds(pl.multiple_of(flip(d) * piece, piece), piece)], part.at[d - 1],
               part_send.at[d - 1], part_recv.at[d - 1], col=flip(d))
        for d in range(1, n_col)
    ]
    for copy in part_copies:
        copy.start()

    near_copies = []
    for p, step in enumerate(OFFSETS):
        target = cell - step
        near_copies.append(remote(
            own.at[col], near.at[p], near_send.at[p], near_recv.at[p],
            cell=jnp.clip(target, 0, n_cell - 1)))
    for p in (0, 3, 1, 2):
        step = OFFSETS[p]
        @pl.when((cell - step >= 0) & (cell - step < n_cell))
        def _():
            near_copies[p].start()

    def cube(buf, send, recv):
        copies, index, held = {}, 0, [0]
        for b in bits:
            for h in list(held):
                slot = flip(h)
                copies[h, b] = remote(buf.at[slot], buf.at[slot], send.at[index], recv.at[index], col=flip(b))
                index += 1
            held += [h ^ b for h in held]
        return copies

    own_copies = cube(own, own_send, own_recv)
    side_copies = cube(beside, side_send, side_recv)

    def begin(copies, h):
        for (held, b), copy in copies.items():
            if held == h:
                copy.start()

    def arrive(copies, h):
        for (held, b), copy in copies.items():
            if held ^ b == h:
                copy.wait_recv()

    def forward_order():
        held = [0]
        for b in bits:
            held += [h ^ b for h in held]
        return held

    order = forward_order()

    begin(own_copies, 0)

    for copy in part_copies:
        copy.wait_recv()
    total = ppt[pl.ds(pl.multiple_of(col * piece, piece), piece), :]
    for d in range(1, n_col):
        total = total + part[d - 1]
    table[cell] = total
    table_copies = [
        remote(table.at[cell], table.at[cell], table_send.at[d - 1], table_recv.at[d - 1],
               cell=lax.rem(cell + d, n_cell))
        for d in range(1, n_cell)
    ]
    for copy in table_copies:
        copy.start()

    def product(tile, buf, slot):
        block = buf[slot]
        for h in range(2):
            columns = pl.ds(pl.multiple_of(slot * rows + h * half, half), half)
            acc[h] += jnp.dot(tiles[tile, :, columns], block, preferred_element_type=F32)

    loads[2].wait()
    acc[...] = jnp.zeros_like(acc)
    product(0, own, col)
    for h in order[1:]:
        arrive(own_copies, h)
        begin(own_copies, h)
        if h == bits[0]:
            for p, step in enumerate(OFFSETS):
                @pl.when((cell + step >= 0) & (cell + step < n_cell))
                def _():
                    near_copies[p].wait_recv()
            offset = offset_ref[cell]
            position = offset + 2 - (offset > 0).astype(jnp.int32)
            picked = near[position]
            beside[col] = jnp.where(count_ref[cell] == 2, picked, jnp.zeros_like(picked))
            begin(side_copies, 0)
        product(0, own, flip(h))

    for copy in table_copies:
        copy.wait_recv()
    loads[3].wait()
    used = fcount_ref[cell]
    mixed = jnp.zeros((piece, width), F32)
    for k in range(cores.shape[0]):
        source = table[fsrc_ref[cell, k]]
        source = jnp.where(k < used, source, jnp.zeros_like(source))
        mixed = mixed + lax.dot_general(
            source, cores[k], (((1,), (1,)), ((), ())),
            precision=lax.Precision.HIGHEST, preferred_element_type=F32)
    mine = pl.ds(pl.multiple_of(col * piece, piece), piece)
    coret[mine, :] = mixed.astype(BF16)
    core_copies = [
        remote(coret.at[mine], coret.at[mine], core_send.at[d - 1], core_recv.at[d - 1], col=flip(d))
        for d in range(1, n_col)
    ]
    for copy in core_copies:
        copy.start()

    loads[5].wait()
    product(1, beside, col)
    for h in order[1:]:
        arrive(side_copies, h)
        begin(side_copies, h)
        product(1, beside, flip(h))

    loads[4].wait()
    for copy in core_copies:
        copy.wait_recv()
    far = lax.dot_general(bout[...], coret[...], (((1,), (1,)), ((), ())), preferred_element_type=F32)
    out_ref[...] = acc[0][:, :width] + acc[1][:, width:] + far

    for copy in part_copies + table_copies + core_copies:
        copy.wait_send()
    for copy in list(own_copies.values()) + list(side_copies.values()):
        copy.wait_send()
    for p, step in enumerate(OFFSETS):
        @pl.when((cell - step >= 0) & (cell - step < n_cell))
        def _():
            near_copies[p].wait_send()


def body(
    n_cell, n_col,
    grad, near_tiles, tile_count, near_offset, far_src, far_count, far_cores, basis_out, basis_in
):
    rows, width = grad.shape
    slots, _, clus = near_tiles.shape[1:]
    far, rank = far_cores.shape[1:3]
    half, piece = rows // 2, width // n_col
    dma = lambda n: pltpu.SemaphoreType.DMA((max(n, 1),))
    smem = pl.BlockSpec(memory_space=pltpu.SMEM)
    anywhere = pl.BlockSpec(memory_space=pl.ANY)
    return pl.pallas_call(
        functools.partial(kernel, n_cell, n_col),
        out_shape=jax.ShapeDtypeStruct((rows, width), F32),
        in_specs=[smem] * 4 + [anywhere] * 5,
        out_specs=pl.BlockSpec(memory_space=pltpu.VMEM),
        scratch_shapes=[
            pltpu.VMEM((rows, width), F32),
            pltpu.VMEM((slots, rows, clus), BF16),
            pltpu.VMEM((far, rank, rank), F32),
            pltpu.VMEM((rows, rank), BF16),
            pltpu.VMEM((rows, rank), BF16),
            pltpu.VMEM((n_col, half, 2 * width), BF16),
            pltpu.VMEM((len(OFFSETS), half, 2 * width), BF16),
            pltpu.VMEM((n_col, half, 2 * width), BF16),
            pltpu.VMEM((width, rank), F32),
            pltpu.VMEM((n_col - 1, piece, rank), F32),
            pltpu.VMEM((n_cell, piece, rank), F32),
            pltpu.VMEM((width, rank), BF16),
            pltpu.VMEM((2, rows, 2 * width), F32),
            dma(6),
            dma(n_col - 1), dma(n_col - 1),
            dma(len(OFFSETS)), dma(len(OFFSETS)),
            dma(n_col - 1), dma(n_col - 1),
            dma(n_col - 1), dma(n_col - 1),
            dma(n_cell - 1), dma(n_cell - 1),
            dma(n_col - 1), dma(n_col - 1),
        ],
        compiler_params=pltpu.CompilerParams(
            collective_id=0, has_side_effects=True, vmem_limit_bytes=48 * 1024 * 1024
        ),
    )(tile_count, near_offset, far_src, far_count, grad, near_tiles, far_cores, basis_out, basis_in)


def solution(mesh):
    placed = (
        P(("chain", "cell", "col"), None),
        P("cell", None, "col", None),
        P(),
        P(),
        P(),
        P(),
        P("cell", None, None, None),
        P(("cell", "col"), None),
        P(("cell", "col"), None),
    )
    return jax.shard_map(
        functools.partial(body, mesh.shape["cell"], mesh.shape["col"]),
        mesh=mesh,
        in_specs=placed,
        out_specs=P(("chain", "cell", "col"), None),
        check_vma=False,
    )
```

time: 61.3 us -> 26 us (0.42)
  blocking collectives: 32.9 us -> 0 us
  Pallas kernels: 0 us -> 16.1 us
  starting transfers between devices: 10.6 us -> 0 us
  matrix products: 7.95 us -> 0 us
  local copies, waits for them, and re-layouts: 4.33 us -> 9.5 us
  other arithmetic: 2.98 us -> 0 us
  between operations: 2.04 us -> 0.04 us
    all_gather x2 -> x0, blocking collectives: 21.5 us -> none  [the longest x1 14.3 us: body(): table = lax.all_gather(proj[None], 'cell', axis=0, tiled=True)]
    pallas_call x0 -> x1, Pallas kernels: none -> 16.1 us  [body(): pl.pallas_call(functools.partial(kernel, n_cell, n_col), out_shape=jax.Sh...]
    psum x1 -> x0, blocking collectives: 11.4 us -> none  [body(): proj = lax.psum(partial_proj, 'col')]
    ppermute x4 -> x0, starting transfers between devices: 10.6 us -> none  [shifted(): return lax.ppermute(value, axis, pairs)]
    unnamed x2 -> x15, local copies, waits for them, and re-layouts: 0.01 us -> 8.72 us
    dot_general x5 -> x0, matrix products: 7.95 us -> none  [the longest x1 3.02 us: body(): own_term = jnp.dot(tiles[0], whole, preferred_element_type=jnp.float32)]
    dynamic_slice x3 -> x0, local copies, waits for them, and re-layouts: 3.76 us -> none  [the longest x1 1.27 us: body(): tile_count[owner] == 2]
    and x1 -> x0, other arithmetic: 1.34 us -> none  [coupling(): picked = jnp.take(table, sources, axis=0)]
  transfers between devices with their start and end apart: 4 -> 0, of which waited for: 0 -> 0; matrix products, arithmetic and copies ran while one was open for 15% -> 0% of each run, Pallas kernels for 0% -> 0%
where the time goes in v1:
time: 26 us; the launch traced here: 25.7 us
  Pallas kernels  16.1 us (62%)
  local copies, waits for them, and re-layouts  9.5 us (37%)
    pallas_call x1, Pallas kernels, body(): pl.pallas_call(functools.partial(kernel, n_cell, n_col), out_shape=jax.Sh...  16.1 us
    unnamed x15, local copies, waits for them, and re-layouts  8.72 us
    pallas_call x1, local copies, waits for them, and re-layouts, body(): pl.pallas_call(functools.partial(kernel, n_cell, n_col), out_shape=jax.Sh...  0.77 us

profile of v1, /device:TPU:0, one launch (start us, length us, event | category | flops | bytes accessed | tf_op | source)
XLA Modules:
  0.0 25.7 jit_solution(14069206699356410051)
XLA Ops:
  0.0 1.0 %copy.11.bout_hbm = bf16[512,64]{1,0:T(8,128)(2,1)S(1)} copy(bf16[512,64]{0,1:T(8,128)(2,1)} %param.16) | data formatting | bytes 131072 | tf_op args[7]
  1.0 1.0 %copy.12.bin_hbm = bf16[512,64]{1,0:T(8,128)(2,1)S(1)} copy(bf16[512,64]{0,1:T(8,128)(2,1)} %param.17) | data formatting | bytes 131072 | tf_op args[8]
  1.9 1.0 %copy.10.grad_hbm = f32[512,64]{1,0:T(8,128)S(1)} copy(f32[512,64]{0,1:T(8,128)} %param.9) | data formatting | bytes 262144 | tf_op args[0]
  3.0 0.0 copy-start
  3.0 2.2 %copy-done = bf16[1,2,512,2048]{3,2,1,0:T(8,128)(2,1)S(1)} copy-done((bf16[1,2,512,2048]{3,2,1,0:T(8,128)(2,1)S(1)}, bf16[1,2,512,2048]{3,2,1,0:T(8,128)(2,1)}, u32[]{:S(2)}) %copy-start) | copy-done | bytes 4194328
  5.2 0.0 copy-start.1
  5.2 0.9 %copy-done.1 = f32[1,8,64,64]{3,2,1,0:T(8,128)S(1)} copy-done((f32[1,8,64,64]{3,2,1,0:T(8,128)S(1)}, f32[1,8,64,64]{3,2,1,0:T(8,128)}, u32[]{:S(2)}) %copy-start.1) | copy-done | bytes 131096
  6.1 0.0 copy-start.2
  6.1 0.7 %copy-done.2 = s32[4,8]{1,0:T(4,128)S(1)} copy-done((s32[4,8]{1,0:T(4,128)S(1)}, s32[4,8]{1,0:T(4,128)}, u32[]{:S(2)}) %copy-start.2) | copy-done | bytes 152
  6.8 0.0 copy-start.3
  6.8 0.7 %copy-done.3 = s32[4]{0:T(128)S(1)} copy-done((s32[4]{0:T(128)S(1)}, s32[4]{0:T(128)}, u32[]{:S(2)}) %copy-start.3) | copy-done | bytes 40
  7.4 0.0 copy-start.4
  7.5 0.7 %copy-done.4 = s32[4]{0:T(128)S(1)} copy-done((s32[4]{0:T(128)S(1)}, s32[4]{0:T(128)}, u32[]{:S(2)}) %copy-start.4) | copy-done | bytes 40
  8.1 0.0 copy-start.5
  8.1 0.7 %copy-done.5 = s32[4]{0:T(128)S(1)} copy-done((s32[4]{0:T(128)S(1)}, s32[4]{0:T(128)}, u32[]{:S(2)}) %copy-start.5) | copy-done | bytes 40
  8.8 16.1 %shard_map.91 = f32[512,64]{1,0:T(8,128)S(1)} custom-call(s32[4]{0:T(128)S(1)} %copy-done.3, s32[4]{0:T(128)S(1)} %copy-done.4, s32[4,8]{1,0:T(4,128)S(1)} %copy-done.2, s32[4]{0:T(128)S(1)} %copy-done.5, f32[512,64]{1,0:T(8,128)S(1)} %copy.10.grad_hbm, bf16[1,2,512,2048]{3,2,1,0:T(8,128)(2,1)S(1)} %copy-done, f32[1,8,64,64]{3,2,1,0:T(8,128)S(1)} %copy-done.1, ...), custom_call_target="tpu_custom_call" | custom-call | tf_op jit(solution)/shard_map/pallas_call | solution.py:221
  24.9 0.8 %copy.13 = f32[512,64]{0,1:T(8,128)} copy(f32[512,64]{1,0:T(8,128)S(1)} %shard_map.91) | data formatting | bytes 262144 | tf_op jit(solution)/shard_map/pallas_call | solution.py:221
Async XLA Ops:
  3.0 2.2 %copy-start = (bf16[1,2,512,2048]{3,2,1,0:T(8,128)(2,1)S(1)}, bf16[1,2,512,2048]{3,2,1,0:T(8,128)(2,1)}, u32[]{:S(2)}) copy-start(bf16[1,2,512,2048]{3,2,1,0:T(8,128)(2,1)} %tiles_hbm.1) | copy-start | bytes 12582916
  5.2 0.9 %copy-start.1 = (f32[1,8,64,64]{3,2,1,0:T(8,128)S(1)}, f32[1,8,64,64]{3,2,1,0:T(8,128)}, u32[]{:S(2)}) copy-start(f32[1,8,64,64]{3,2,1,0:T(8,128)} %cores_hbm.1) | copy-start | bytes 393220
  6.1 0.7 %copy-start.2 = (s32[4,8]{1,0:T(4,128)S(1)}, s32[4,8]{1,0:T(4,128)}, u32[]{:S(2)}) copy-start(s32[4,8]{1,0:T(4,128)} %fsrc_ref.1) | copy-start | bytes 388
  6.8 0.7 %copy-start.3 = (s32[4]{0:T(128)S(1)}, s32[4]{0:T(128)}, u32[]{:S(2)}) copy-start(s32[4]{0:T(128)} %count_ref.1) | copy-start | bytes 52
  7.4 0.7 %copy-start.4 = (s32[4]{0:T(128)S(1)}, s32[4]{0:T(128)}, u32[]{:S(2)}) copy-start(s32[4]{0:T(128)} %offset_ref.1) | copy-start | bytes 52
  8.1 0.7 %copy-start.5 = (s32[4]{0:T(128)S(1)}, s32[4]{0:T(128)}, u32[]{:S(2)}) copy-start(s32[4]{0:T(128)} %fcount_ref.1) | copy-start | bytes 52

commit v2 on v1

v2 whole, which is shorter than its diff:
```python
import functools

import jax
import jax.numpy as jnp
from jax import lax
from jax.experimental import pallas as pl
from jax.experimental.pallas import tpu as pltpu
from jax.sharding import PartitionSpec as P

MESH = pl.DeviceIdType.MESH
OFFSETS = (-2, -1, 1, 2)
CHUNKS = 2
F32 = jnp.float32
BF16 = jnp.bfloat16


def remote(src, dst, send, recv, **where):
    return pltpu.make_async_remote_copy(
        src_ref=src, dst_ref=dst, send_sem=send, recv_sem=recv, device_id=where, device_id_type=MESH
    )


def across(a, b, **kw):
    return lax.dot_general(a, b, (((1,), (1,)), ((), ())), preferred_element_type=F32, **kw)


def kernel(
    n_cell, n_col,
    count_hbm, offset_hbm, fsrc_hbm, fcount_hbm, grad_hbm, tiles_hbm, cores_hbm, bout_hbm, bin_hbm,
    out_ref,
    count_ref, offset_ref, fsrc_ref, fcount_ref,
    grad, tiles, cores, bout, bin_,
    own, near, beside, ppt, part, table, flat, coret, acc,
    local_sem, own_send, own_recv, near_send, near_recv, side_send, side_recv,
    part_send, part_recv, table_send, table_recv, core_send, core_recv,
):
    cell = lax.axis_index("cell")
    col = lax.axis_index("col")
    width, rows = grad.shape
    size = rows // CHUNKS
    piece = width // n_col
    bits = [1 << b for b in reversed(range(n_col.bit_length() - 1))]

    def flip(d):
        value = col
        for b in bits:
            if d & b:
                value = value + b - 2 * b * lax.rem(value // b, 2)
        return value

    barrier = pltpu.get_barrier_semaphore()
    for d in range(1, n_col):
        pl.semaphore_signal(barrier, inc=1, device_id={"col": flip(d)}, device_id_type=MESH)
    for d in range(1, n_cell):
        pl.semaphore_signal(
            barrier, inc=1, device_id={"cell": lax.rem(cell + d, n_cell)}, device_id_type=MESH
        )

    pairs = {
        "grad": (grad_hbm, grad), "bin": (bin_hbm, bin_),
        "count": (count_hbm, count_ref), "offset": (offset_hbm, offset_ref),
        "fsrc": (fsrc_hbm, fsrc_ref), "fcount": (fcount_hbm, fcount_ref),
        "cores": (cores_hbm.at[0], cores), "tile0": (tiles_hbm.at[0, 0], tiles.at[0]),
        "bout": (bout_hbm, bout), "tile1": (tiles_hbm.at[0, 1], tiles.at[1]),
    }
    loads = {
        name: pltpu.make_async_copy(src, dst, local_sem.at[i])
        for i, (name, (src, dst)) in enumerate(pairs.items())
    }
    for load in loads.values():
        load.start()

    loads["grad"].wait()
    rounded = grad[...].astype(BF16)
    for q in range(CHUNKS):
        own[col, q] = rounded[:, q * size:(q + 1) * size]
    loads["bin"].wait()
    ppt[...] = across(rounded, bin_[...])
    for p, step in enumerate(OFFSETS):
        @pl.when((cell + step < 0) | (cell + step >= n_cell))
        def _():
            near[p] = jnp.zeros(near.shape[1:], BF16)
    loads["cores"].wait()
    rank = cores.shape[1]
    for k in range(0, cores.shape[0], 2):
        flat[:, k * rank:(k + 2) * rank] = jnp.concatenate([cores[k], cores[k + 1]], axis=1)
    for name in ("count", "offset", "fsrc", "fcount"):
        loads[name].wait()

    pl.semaphore_wait(barrier, (n_col - 1) + (n_cell - 1))

    part_copies = [
        remote(ppt.at[pl.ds(pl.multiple_of(flip(d) * piece, piece), piece)], part.at[d - 1],
               part_send.at[d - 1], part_recv.at[d - 1], col=flip(d))
        for d in range(1, n_col)
    ]
    for copy in part_copies:
        copy.start()

    near_copies = {}
    for q in range(CHUNKS):
        for p, step in enumerate(OFFSETS):
            index = q * len(OFFSETS) + p
            near_copies[q, p] = remote(
                own.at[col, q], near.at[p, q], near_send.at[index], near_recv.at[index],
                cell=jnp.clip(cell - step, 0, n_cell - 1))
    for q in range(CHUNKS):
        for p in (0, 3, 1, 2):
            step = OFFSETS[p]
            @pl.when((cell - step >= 0) & (cell - step < n_cell))
            def _():
                near_copies[q, p].start()

    def cube(buf, send, recv):
        copies, index, held = {}, 0, [0]
        for b in bits:
            for h in list(held):
                slot = flip(h)
                for q in range(CHUNKS):
                    copies[h, q, b] = remote(
                        buf.at[slot, q], buf.at[slot, q], send.at[index], recv.at[index], col=flip(b))
                    index += 1
            held += [h ^ b for h in held]
        return copies, held

    own_copies, order = cube(own, own_send, own_recv)
    side_copies, _ = cube(beside, side_send, side_recv)

    def begin(copies, h, q):
        for (held, chunk, b), copy in copies.items():
            if held == h and chunk == q:
                copy.start()

    def arrive(copies, h, q):
        for (held, chunk, b), copy in copies.items():
            if held ^ b == h and chunk == q:
                copy.wait_recv()

    for q in range(CHUNKS):
        begin(own_copies, 0, q)

    def product(tile, buf, slot, q):
        columns = pl.ds(pl.multiple_of(slot * rows + q * size, size), size)
        acc[...] += across(buf[slot, q], tiles[tile, :, columns])

    acc[...] = jnp.zeros_like(acc)
    loads["tile0"].wait()
    for q in range(CHUNKS):
        product(0, own, col, q)

    for copy in part_copies:
        copy.wait_recv()
    total = ppt[pl.ds(pl.multiple_of(col * piece, piece), piece), :]
    for d in range(1, n_col):
        total = total + part[d - 1]
    table[cell] = total
    table_copies = [
        remote(table.at[cell], table.at[cell], table_send.at[d - 1], table_recv.at[d - 1],
               cell=lax.rem(cell + d, n_cell))
        for d in range(1, n_cell)
    ]
    for copy in table_copies:
        copy.start()

    for h in order[1:]:
        for q in range(CHUNKS):
            arrive(own_copies, h, q)
            begin(own_copies, h, q)
        if h == bits[0]:
            for q in range(CHUNKS):
                product(0, own, flip(h), q)

    offset = offset_ref[cell]
    position = offset + 2 - (offset > 0).astype(jnp.int32)
    use = count_ref[cell] == 2
    for q in range(CHUNKS):
        for p, step in enumerate(OFFSETS):
            @pl.when((cell + step >= 0) & (cell + step < n_cell))
            def _():
                near_copies[q, p].wait_recv()
        if q == CHUNKS - 1:
            for c in range(CHUNKS):
                picked = near[position, c]
                beside[col, c] = jnp.where(use, picked, jnp.zeros_like(picked))
                begin(side_copies, 0, c)

    for copy in table_copies:
        copy.wait_recv()
    used = fcount_ref[cell]
    picks = []
    for k in range(cores.shape[0]):
        source = table[fsrc_ref[cell, k]]
        picks.append(jnp.where(k < used, source, jnp.zeros_like(source)))
    mixed = across(jnp.concatenate(picks, axis=1), flat[...], precision=lax.Precision.HIGHEST)
    mine = pl.ds(pl.multiple_of(col * piece, piece), piece)
    coret[mine, :] = mixed.astype(BF16)
    core_copies = [
        remote(coret.at[mine], coret.at[mine], core_send.at[d - 1], core_recv.at[d - 1], col=flip(d))
        for d in range(1, n_col)
    ]
    for copy in core_copies:
        copy.start()

    for h in order[1:]:
        if h != bits[0]:
            for q in range(CHUNKS):
                product(0, own, flip(h), q)
    loads["tile1"].wait()
    for q in range(CHUNKS):
        product(1, beside, col, q)
    for h in order[1:]:
        for q in range(CHUNKS):
            arrive(side_copies, h, q)
            begin(side_copies, h, q)
            product(1, beside, flip(h), q)

    loads["bout"].wait()
    for copy in core_copies:
        copy.wait_recv()
    out_ref[...] = acc[...] + jnp.dot(coret[...], bout[...], preferred_element_type=F32)

    for copy in part_copies + table_copies + core_copies:
        copy.wait_send()
    for copy in list(own_copies.values()) + list(side_copies.values()):
        copy.wait_send()
    for q in range(CHUNKS):
        for p, step in enumerate(OFFSETS):
            @pl.when((cell - step >= 0) & (cell - step < n_cell))
            def _():
                near_copies[q, p].wait_send()


def body(
    n_cell, n_col,
    grad, near_tiles, tile_count, near_offset, far_src, far_count, far_cores, basis_out, basis_in
):
    rows, width = grad.shape
    slots, _, clus = near_tiles.shape[1:]
    far, rank = far_cores.shape[1:3]
    size, piece = rows // CHUNKS, width // n_col
    dma = lambda n: pltpu.SemaphoreType.DMA((max(n, 1),))
    hbm = pl.BlockSpec(memory_space=pltpu.HBM)
    out = pl.pallas_call(
        functools.partial(kernel, n_cell, n_col),
        out_shape=jax.ShapeDtypeStruct((width, rows), F32),
        in_specs=[hbm] * 9,
        out_specs=pl.BlockSpec(memory_space=pltpu.VMEM),
        scratch_shapes=[
            pltpu.SMEM(tile_count.shape, jnp.int32),
            pltpu.SMEM(near_offset.shape, jnp.int32),
            pltpu.SMEM(far_src.shape, jnp.int32),
            pltpu.SMEM(far_count.shape, jnp.int32),
            pltpu.VMEM((width, rows), F32),
            pltpu.VMEM((slots, rows, clus), BF16),
            pltpu.VMEM((far, rank, rank), F32),
            pltpu.VMEM((rank, rows), BF16),
            pltpu.VMEM((rank, rows), BF16),
            pltpu.VMEM((n_col, CHUNKS, width, size), BF16),
            pltpu.VMEM((len(OFFSETS), CHUNKS, width, size), BF16),
            pltpu.VMEM((n_col, CHUNKS, width, size), BF16),
            pltpu.VMEM((width, rank), F32),
            pltpu.VMEM((n_col - 1, piece, rank), F32),
            pltpu.VMEM((n_cell, piece, rank), F32),
            pltpu.VMEM((rank, far * rank), F32),
            pltpu.VMEM((width, rank), BF16),
            pltpu.VMEM((width, rows), F32),
            dma(10),
            dma((n_col - 1) * CHUNKS), dma((n_col - 1) * CHUNKS),
            dma(len(OFFSETS) * CHUNKS), dma(len(OFFSETS) * CHUNKS),
            dma((n_col - 1) * CHUNKS), dma((n_col - 1) * CHUNKS),
            dma(n_col - 1), dma(n_col - 1),
            dma(n_cell - 1), dma(n_cell - 1),
            dma(n_col - 1), dma(n_col - 1),
        ],
        compiler_params=pltpu.CompilerParams(
            collective_id=0, has_side_effects=True, vmem_limit_bytes=63 * 1024 * 1024
        ),
    )(tile_count, near_offset, far_src, far_count, grad.T, near_tiles, far_cores, basis_out.T, basis_in.T)
    return out.T


def solution(mesh):
    placed = (
        P(("chain", "cell", "col"), None),
        P("cell", None, "col", None),
        P(),
        P(),
        P(),
        P(),
        P("cell", None, None, None),
        P(("cell", "col"), None),
        P(("cell", "col"), None),
    )
    return jax.shard_map(
        functools.partial(body, mesh.shape["cell"], mesh.shape["col"]),
        mesh=mesh,
        in_specs=placed,
        out_specs=P(("chain", "cell", "col"), None),
        check_vma=False,
    )
```

time: 26 us -> 18 us (0.69)
  local copies, waits for them, and re-layouts: 9.5 us -> 1.57 us
    unnamed x15 -> x1, local copies, waits for them, and re-layouts: 8.72 us -> 1.57 us
    pallas_call x1 -> x0, local copies, waits for them, and re-layouts: 0.77 us -> none  [body(): pl.pallas_call(functools.partial(kernel, n_cell, n_col), out_shape=jax.Sh...]
where the time goes in v2:
time: 18 us; the launch traced here: 17.7 us
  Pallas kernels  16.1 us (89%)
  local copies, waits for them, and re-layouts  1.57 us (9%)
    pallas_call x1, Pallas kernels, body(): pl.pallas_call(functools.partial(kernel, n_cell, n_col), out_shape=jax.Sh...  16.1 us
    unnamed x1, local copies, waits for them, and re-layouts  1.57 us

profile of v2, /device:TPU:0, one launch (start us, length us, event | category | flops | bytes accessed | tf_op | source)
XLA Modules:
  0.0 17.7 jit_solution(831310226636342572)
XLA Ops:
  0.0 16.1 %shard_map.91 = f32[64,512]{1,0:T(8,128)} custom-call(s32[4]{0:T(128)} %count_hbm.1, s32[4]{0:T(128)} %offset_hbm.1, s32[4,8]{1,0:T(4,128)} %fsrc_hbm.1, s32[4]{0:T(128)} %fcount_hbm.1, f32[64,512]{1,0:T(8,128)} %bitcast.5, bf16[1,2,512,2048]{3,2,1,0:T(8,128)(2,1)} %tiles_hbm.1, f32[1,8,64,64]{3,2,1,0:T(8,128)} %cores_hbm.1, bf16[64,512]{1,0:T(8,128)(2,1)} %bitcast.6, ...), custom_call_target="tpu_custom_call" | custom-call | tf_op jit(solution)/shard_map/pallas_call | solution.py:243
  16.1 1.6 %copy.11 = f32[512,64]{0,1:T(8,128)} copy(f32[512,64]{0,1:T(8,128)} %bitcast.4) | data formatting | bytes 262144

commit v3 on v2

--- a/solution.py
+++ b/solution.py
@@ -67,49 +67,38 @@
         name: pltpu.make_async_copy(src, dst, local_sem.at[i])
         for i, (name, (src, dst)) in enumerate(pairs.items())
     }
-    for load in loads.values():
-        load.start()
-
-    loads["grad"].wait()
-    rounded = grad[...].astype(BF16)
-    for q in range(CHUNKS):
-        own[col, q] = rounded[:, q * size:(q + 1) * size]
-    loads["bin"].wait()
-    ppt[...] = across(rounded, bin_[...])
+    for name in ("grad", "bin", "count", "offset"):
+        loads[name].start()
+
     for p, step in enumerate(OFFSETS):
         @pl.when((cell + step < 0) | (cell + step >= n_cell))
         def _():
             near[p] = jnp.zeros(near.shape[1:], BF16)
-    loads["cores"].wait()
-    rank = cores.shape[1]
-    for k in range(0, cores.shape[0], 2):
-        flat[:, k * rank:(k + 2) * rank] = jnp.concatenate([cores[k], cores[k + 1]], axis=1)
-    for name in ("count", "offset", "fsrc", "fcount"):
-        loads[name].wait()
-
-    pl.semaphore_wait(barrier, (n_col - 1) + (n_cell - 1))
-
-    part_copies = [
-        remote(ppt.at[pl.ds(pl.multiple_of(flip(d) * piece, piece), piece)], part.at[d - 1],
-               part_send.at[d - 1], part_recv.at[d - 1], col=flip(d))
-        for d in range(1, n_col)
-    ]
-    for copy in part_copies:
-        copy.start()
-
-    near_copies = {}
-    for q in range(CHUNKS):
-        for p, step in enumerate(OFFSETS):
+    loads["grad"].wait()
+    rounded = grad[...].astype(BF16)
+    for q in range(CHUNKS):
+        own[col, q] = rounded[:, q * size:(q + 1) * size]
+
+    up, down = jnp.minimum(cell + 1, n_cell - 1), jnp.maximum(cell - 1, 0)
+    below, above = cell > 0, cell < n_cell - 1
+    inner = below & above
+    near_copies, near_when = {}, {}
+    for q in range(CHUNKS):
+        for p, src, target, when in (
+            (0, near.at[1, q], up, inner), (1, own.at[col, q], up, above),
+            (2, own.at[col, q], down, below), (3, near.at[2, q], down, inner),
+        ):
             index = q * len(OFFSETS) + p
             near_copies[q, p] = remote(
-                own.at[col, q], near.at[p, q], near_send.at[index], near_recv.at[index],
-                cell=jnp.clip(cell - step, 0, n_cell - 1))
-    for q in range(CHUNKS):
-        for p in (0, 3, 1, 2):
-            step = OFFSETS[p]
-            @pl.when((cell - step >= 0) & (cell - step < n_cell))
-            def _():
-                near_copies[q, p].start()
+                src, near.at[p, q], near_send.at[index], near_recv.at[index], cell=target)
+            near_when[p] = when
+
+    def near_start(q, p):
+        pl.when(near_when[p])(near_copies[q, p].start)
+
+    def near_arrive(q, p):
+        step = OFFSETS[p]
+        pl.when((cell + step >= 0) & (cell + step < n_cell))(near_copies[q, p].wait_recv)
 
     def cube(buf, send, recv):
         copies, index, held = {}, 0, [0]
@@ -136,18 +125,34 @@
             if held ^ b == h and chunk == q:
                 copy.wait_recv()
 
-    for q in range(CHUNKS):
+    pl.semaphore_wait(barrier, (n_col - 1) + (n_cell - 1))
+
+    def first(q):
+        near_start(q, 1)
+        near_start(q, 2)
         begin(own_copies, 0, q)
+
+    first(0)
+    loads["bin"].wait()
+    ppt[...] = across(rounded, bin_[...])
+    part_copies = [
+        remote(ppt.at[pl.ds(pl.multiple_of(flip(d) * piece, piece), piece)], part.at[d - 1],
+               part_send.at[d - 1], part_recv.at[d - 1], col=flip(d))
+        for d in range(1, n_col)
+    ]
+    for copy in part_copies:
+        copy.start()
+
+    for q in range(1, CHUNKS):
+        first(q)
+    for name in ("tile0", "cores", "fsrc", "fcount", "tile1", "bout"):
+        loads[name].start()
 
     def product(tile, buf, slot, q):
         columns = pl.ds(pl.multiple_of(slot * rows + q * size, size), size)
         acc[...] += across(buf[slot, q], tiles[tile, :, columns])
 
     acc[...] = jnp.zeros_like(acc)
-    loads["tile0"].wait()
-    for q in range(CHUNKS):
-        product(0, own, col, q)
-
     for copy in part_copies:
         copy.wait_recv()
     total = ppt[pl.ds(pl.multiple_of(col * piece, piece), piece), :]
@@ -162,6 +167,14 @@
     for copy in table_copies:
         copy.start()
 
+    for q in range(CHUNKS):
+        near_arrive(q, 1)
+        near_start(q, 0)
+        near_arrive(q, 2)
+        near_start(q, 3)
+    loads["tile0"].wait()
+    for q in range(CHUNKS):
+        product(0, own, col, q)
     for h in order[1:]:
         for q in range(CHUNKS):
             arrive(own_copies, h, q)
@@ -170,19 +183,22 @@
             for q in range(CHUNKS):
                 product(0, own, flip(h), q)
 
+    for name in ("cores", "fsrc", "fcount", "count", "offset"):
+        loads[name].wait()
+    rank = cores.shape[1]
+    for k in range(0, cores.shape[0], 2):
+        flat[:, k * rank:(k + 2) * rank] = jnp.concatenate([cores[k], cores[k + 1]], axis=1)
+
     offset = offset_ref[cell]
-    position = offset + 2 - (offset > 0).astype(jnp.int32)
     use = count_ref[cell] == 2
     for q in range(CHUNKS):
+        near_arrive(q, 0)
+        near_arrive(q, 3)
+        picked = jnp.zeros(near.shape[2:], BF16)
         for p, step in enumerate(OFFSETS):
-            @pl.when((cell + step >= 0) & (cell + step < n_cell))
-            def _():
-                near_copies[q, p].wait_recv()
-        if q == CHUNKS - 1:
-            for c in range(CHUNKS):
-                picked = near[position, c]
-                beside[col, c] = jnp.where(use, picked, jnp.zeros_like(picked))
-                begin(side_copies, 0, c)
+            picked = jnp.where(use & (offset == step), near[p, q], picked)
+        beside[col, q] = picked
+        begin(side_copies, 0, q)
 
     for copy in table_copies:
         copy.wait_recv()
@@ -223,11 +239,8 @@
         copy.wait_send()
     for copy in list(own_copies.values()) + list(side_copies.values()):
         copy.wait_send()
-    for q in range(CHUNKS):
-        for p, step in enumerate(OFFSETS):
-            @pl.when((cell - step >= 0) & (cell - step < n_cell))
-            def _():
-                near_copies[q, p].wait_send()
+    for (_, p), copy in near_copies.items():
+        pl.when(near_when[p])(copy.wait_send)
 
 
 def body(
@@ -242,7 +255,7 @@
     hbm = pl.BlockSpec(memory_space=pltpu.HBM)
     out = pl.pallas_call(
         functools.partial(kernel, n_cell, n_col),
-        out_shape=jax.ShapeDtypeStruct((width, rows), F32),
+        out_shape=pltpu.VMEM((width, rows), F32),
         in_specs=[hbm] * 9,
         out_specs=pl.BlockSpec(memory_space=pltpu.VMEM),
         scratch_shapes=[
@@ -273,7 +286,7 @@
             dma(n_col - 1), dma(n_col - 1),
         ],
         compiler_params=pltpu.CompilerParams(
-            collective_id=0, has_side_effects=True, vmem_limit_bytes=63 * 1024 * 1024
+            collective_id=0, has_side_effects=True, vmem_limit_bytes=56 * 1024 * 1024
         ),
     )(tile_count, near_offset, far_src, far_count, grad.T, near_tiles, far_cores, basis_out.T, basis_in.T)
     return out.T

time: 18 us -> 17.2 us (0.956)
  local copies, waits for them, and re-layouts: 1.57 us -> 0.66 us
    unnamed x1, local copies, waits for them, and re-layouts: 1.57 us -> 0.66 us
where the time goes in v3:
time: 17.2 us; the launch traced here: 16.9 us
  Pallas kernels  16.2 us (94%)
  local copies, waits for them, and re-layouts  0.66 us (4%)
    pallas_call x1, Pallas kernels, body(): pl.pallas_call(functools.partial(kernel, n_cell, n_col), out_shape=pltpu....  16.2 us
    unnamed x1, local copies, waits for them, and re-layouts  0.66 us

profile of v3, /device:TPU:0, one launch (start us, length us, event | category | flops | bytes accessed | tf_op | source)
XLA Modules:
  0.0 16.9 jit_solution(15185896378066007242)
XLA Ops:
  0.0 16.2 %shard_map.91 = f32[64,512]{1,0:T(8,128)S(1)} custom-call(s32[4]{0:T(128)} %count_hbm.1, s32[4]{0:T(128)} %offset_hbm.1, s32[4,8]{1,0:T(4,128)} %fsrc_hbm.1, s32[4]{0:T(128)} %fcount_hbm.1, f32[64,512]{1,0:T(8,128)} %bitcast.5, bf16[1,2,512,2048]{3,2,1,0:T(8,128)(2,1)} %tiles_hbm.1, f32[1,8,64,64]{3,2,1,0:T(8,128)} %cores_hbm.1, bf16[64,512]{1,0:T(8,128)(2,1)} %bitcast.6, ...), custom_call_target="tpu_custom_call" | custom-call | tf_op jit(solution)/shard_map/pallas_call | solution.py:256
  16.2 0.7 %copy.11 = f32[512,64]{0,1:T(8,128)} copy(f32[512,64]{0,1:T(8,128)S(1)} %bitcast.4) | data formatting | bytes 262144

commit v4 on v3

--- a/solution.py
+++ b/solution.py
@@ -27,10 +27,10 @@
 def kernel(
     n_cell, n_col,
     count_hbm, offset_hbm, fsrc_hbm, fcount_hbm, grad_hbm, tiles_hbm, cores_hbm, bout_hbm, bin_hbm,
-    out_ref,
+    acc,
     count_ref, offset_ref, fsrc_ref, fcount_ref,
     grad, tiles, cores, bout, bin_,
-    own, near, beside, ppt, part, table, flat, coret, acc,
+    own, near, beside, ppt, part, table, flat, coret,
     local_sem, own_send, own_recv, near_send, near_recv, side_send, side_recv,
     part_send, part_recv, table_send, table_recv, core_send, core_recv,
 ):
@@ -148,9 +148,12 @@
     for name in ("tile0", "cores", "fsrc", "fcount", "tile1", "bout"):
         loads[name].start()
 
-    def product(tile, buf, slot, q):
-        columns = pl.ds(pl.multiple_of(slot * rows + q * size, size), size)
-        acc[...] += across(buf[slot, q], tiles[tile, :, columns])
+    def product(tile, buf, slot, chunks=range(CHUNKS)):
+        total = acc[...]
+        for q in chunks:
+            columns = pl.ds(pl.multiple_of(slot * rows + q * size, size), size)
+            total = total + across(tiles[tile, :, columns], buf[slot, q])
+        acc[...] = total
 
     acc[...] = jnp.zeros_like(acc)
     for copy in part_copies:
@@ -173,15 +176,13 @@
         near_arrive(q, 2)
         near_start(q, 3)
     loads["tile0"].wait()
-    for q in range(CHUNKS):
-        product(0, own, col, q)
+    product(0, own, col)
     for h in order[1:]:
         for q in range(CHUNKS):
             arrive(own_copies, h, q)
             begin(own_copies, h, q)
         if h == bits[0]:
-            for q in range(CHUNKS):
-                product(0, own, flip(h), q)
+            product(0, own, flip(h))
 
     for name in ("cores", "fsrc", "fcount", "count", "offset"):
         loads[name].wait()
@@ -219,21 +220,22 @@
 
     for h in order[1:]:
         if h != bits[0]:
-            for q in range(CHUNKS):
-                product(0, own, flip(h), q)
+            product(0, own, flip(h))
     loads["tile1"].wait()
-    for q in range(CHUNKS):
-        product(1, beside, col, q)
+    product(1, beside, col)
+    loads["bout"].wait()
+    flipped = bout[...].T
     for h in order[1:]:
         for q in range(CHUNKS):
             arrive(side_copies, h, q)
             begin(side_copies, h, q)
-            product(1, beside, flip(h), q)
-
-    loads["bout"].wait()
-    for copy in core_copies:
-        copy.wait_recv()
-    out_ref[...] = acc[...] + jnp.dot(coret[...], bout[...], preferred_element_type=F32)
+        if h != order[-1]:
+            product(1, beside, flip(h))
+        if h == order[-2]:
+            for copy in core_copies:
+                copy.wait_recv()
+            acc[...] += across(flipped, coret[...])
+    product(1, beside, flip(order[-1]))
 
     for copy in part_copies + table_copies + core_copies:
         copy.wait_send()
@@ -253,9 +255,9 @@
     size, piece = rows // CHUNKS, width // n_col
     dma = lambda n: pltpu.SemaphoreType.DMA((max(n, 1),))
     hbm = pl.BlockSpec(memory_space=pltpu.HBM)
-    out = pl.pallas_call(
+    return pl.pallas_call(
         functools.partial(kernel, n_cell, n_col),
-        out_shape=pltpu.VMEM((width, rows), F32),
+        out_shape=pltpu.VMEM((rows, width), F32),
         in_specs=[hbm] * 9,
         out_specs=pl.BlockSpec(memory_space=pltpu.VMEM),
         scratch_shapes=[
@@ -276,7 +278,6 @@
             pltpu.VMEM((n_cell, piece, rank), F32),
             pltpu.VMEM((rank, far * rank), F32),
             pltpu.VMEM((width, rank), BF16),
-            pltpu.VMEM((width, rows), F32),
             dma(10),
             dma((n_col - 1) * CHUNKS), dma((n_col - 1) * CHUNKS),
             dma(len(OFFSETS) * CHUNKS), dma(len(OFFSETS) * CHUNKS),
@@ -289,7 +290,6 @@
             collective_id=0, has_side_effects=True, vmem_limit_bytes=56 * 1024 * 1024
         ),
     )(tile_count, near_offset, far_src, far_count, grad.T, near_tiles, far_cores, basis_out.T, basis_in.T)
-    return out.T
 
 
 def solution(mesh):

time: 17.2 us -> 17.7 us (1.029); the launches traced: 16.9 us -> 17.6 us
  Pallas kernels: 16.2 us -> 16.8 us
    pallas_call x0 -> x1, local copies, waits for them, and re-layouts: none -> 0.77 us  [body(): pl.pallas_call(functools.partial(kernel, n_cell, n_col), out_shape=pltpu....]
    unnamed x1 -> x0, local copies, waits for them, and re-layouts: 0.66 us -> none
    pallas_call x1, Pallas kernels: 16.2 us -> 16.8 us  [body(): pl.pallas_call(functools.partial(kernel, n_cell, n_col), out_shape=pltpu....]
where the time goes in v4:
time: 17.7 us; the launch traced here: 17.6 us
  Pallas kernels  16.8 us (95%)
  local copies, waits for them, and re-layouts  0.77 us (4%)
    pallas_call x1, Pallas kernels, body(): pl.pallas_call(functools.partial(kernel, n_cell, n_col), out_shape=pltpu....  16.8 us
    pallas_call x1, local copies, waits for them, and re-layouts, body(): pl.pallas_call(functools.partial(kernel, n_cell, n_col), out_shape=pltpu....  0.77 us

profile of v4, /device:TPU:0, one launch (start us, length us, event | category | flops | bytes accessed | tf_op | source)
XLA Modules:
  0.0 17.6 jit_solution(16468685250073764287)
XLA Ops:
  0.0 16.8 %shard_map.91 = f32[512,64]{1,0:T(8,128)S(1)} custom-call(s32[4]{0:T(128)} %count_hbm.1, s32[4]{0:T(128)} %offset_hbm.1, s32[4,8]{1,0:T(4,128)} %fsrc_hbm.1, s32[4]{0:T(128)} %fcount_hbm.1, f32[64,512]{1,0:T(8,128)} %bitcast.3, bf16[1,2,512,2048]{3,2,1,0:T(8,128)(2,1)} %tiles_hbm.1, f32[1,8,64,64]{3,2,1,0:T(8,128)} %cores_hbm.1, bf16[64,512]{1,0:T(8,128)(2,1)} %bitcast.4, ...), custom_call_target="tpu_custom_call" | custom-call | tf_op jit(solution)/shard_map/pallas_call | solution.py:258
  16.8 0.8 %copy.10 = f32[512,64]{0,1:T(8,128)} copy(f32[512,64]{1,0:T(8,128)S(1)} %shard_map.91) | data formatting | bytes 262144 | tf_op jit(solution)/shard_map/pallas_call | solution.py:258

commit v5 on v3

--- a/solution.py
+++ b/solution.py
@@ -27,10 +27,10 @@
 def kernel(
     n_cell, n_col,
     count_hbm, offset_hbm, fsrc_hbm, fcount_hbm, grad_hbm, tiles_hbm, cores_hbm, bout_hbm, bin_hbm,
-    out_ref,
+    acc,
     count_ref, offset_ref, fsrc_ref, fcount_ref,
     grad, tiles, cores, bout, bin_,
-    own, near, beside, ppt, part, table, flat, coret, acc,
+    own, near, beside, ppt, part, table, flat, coret,
     local_sem, own_send, own_recv, near_send, near_recv, side_send, side_recv,
     part_send, part_recv, table_send, table_recv, core_send, core_recv,
 ):
@@ -79,19 +79,14 @@
     for q in range(CHUNKS):
         own[col, q] = rounded[:, q * size:(q + 1) * size]
 
-    up, down = jnp.minimum(cell + 1, n_cell - 1), jnp.maximum(cell - 1, 0)
-    below, above = cell > 0, cell < n_cell - 1
-    inner = below & above
     near_copies, near_when = {}, {}
     for q in range(CHUNKS):
-        for p, src, target, when in (
-            (0, near.at[1, q], up, inner), (1, own.at[col, q], up, above),
-            (2, own.at[col, q], down, below), (3, near.at[2, q], down, inner),
-        ):
+        for p, step in enumerate(OFFSETS):
             index = q * len(OFFSETS) + p
             near_copies[q, p] = remote(
-                src, near.at[p, q], near_send.at[index], near_recv.at[index], cell=target)
-            near_when[p] = when
+                own.at[col, q], near.at[p, q], near_send.at[index], near_recv.at[index],
+                cell=jnp.clip(cell - step, 0, n_cell - 1))
+            near_when[p] = (cell - step >= 0) & (cell - step < n_cell)
 
     def near_start(q, p):
         pl.when(near_when[p])(near_copies[q, p].start)
@@ -100,105 +95,89 @@
         step = OFFSETS[p]
         pl.when((cell + step >= 0) & (cell + step < n_cell))(near_copies[q, p].wait_recv)
 
-    def cube(buf, send, recv):
-        copies, index, held = {}, 0, [0]
-        for b in bits:
-            for h in list(held):
-                slot = flip(h)
-                for q in range(CHUNKS):
-                    copies[h, q, b] = remote(
-                        buf.at[slot, q], buf.at[slot, q], send.at[index], recv.at[index], col=flip(b))
-                    index += 1
-            held += [h ^ b for h in held]
-        return copies, held
-
-    own_copies, order = cube(own, own_send, own_recv)
-    side_copies, _ = cube(beside, side_send, side_recv)
-
-    def begin(copies, h, q):
-        for (held, chunk, b), copy in copies.items():
-            if held == h and chunk == q:
-                copy.start()
-
-    def arrive(copies, h, q):
-        for (held, chunk, b), copy in copies.items():
-            if held ^ b == h and chunk == q:
-                copy.wait_recv()
-
-    pl.semaphore_wait(barrier, (n_col - 1) + (n_cell - 1))
-
-    def first(q):
-        near_start(q, 1)
-        near_start(q, 2)
-        begin(own_copies, 0, q)
-
-    first(0)
-    loads["bin"].wait()
-    ppt[...] = across(rounded, bin_[...])
+    order = list(range(2, n_col)) + [1]
+
+    def spread(buf, send, recv):
+        return {
+            (d, q): remote(
+                buf.at[col, q], buf.at[col, q], send.at[(d - 1) * CHUNKS + q],
+                recv.at[(d - 1) * CHUNKS + q], col=flip(d))
+            for d in range(1, n_col) for q in range(CHUNKS)
+        }
+
+    own_copies = spread(own, own_send, own_recv)
+    side_copies = spread(beside, side_send, side_recv)
     part_copies = [
         remote(ppt.at[pl.ds(pl.multiple_of(flip(d) * piece, piece), piece)], part.at[d - 1],
                part_send.at[d - 1], part_recv.at[d - 1], col=flip(d))
         for d in range(1, n_col)
     ]
+    table_copies = [
+        remote(table.at[cell], table.at[cell], table_send.at[d - 1], table_recv.at[d - 1],
+               cell=lax.rem(cell + d, n_cell))
+        for d in range(1, n_cell)
+    ]
+
+    loads["bin"].wait()
+    ppt[...] = across(rounded, bin_[...])
+    pl.semaphore_wait(barrier, (n_col - 1) + (n_cell - 1))
+
     for copy in part_copies:
         copy.start()
-
-    for q in range(1, CHUNKS):
-        first(q)
+    for p in (0, 3, 1, 2):
+        near_start(0, p)
+    for q in range(CHUNKS):
+        for d in order:
+            own_copies[d, q].start()
     for name in ("tile0", "cores", "fsrc", "fcount", "tile1", "bout"):
         loads[name].start()
 
-    def product(tile, buf, slot, q):
-        columns = pl.ds(pl.multiple_of(slot * rows + q * size, size), size)
-        acc[...] += across(buf[slot, q], tiles[tile, :, columns])
-
-    acc[...] = jnp.zeros_like(acc)
     for copy in part_copies:
         copy.wait_recv()
     total = ppt[pl.ds(pl.multiple_of(col * piece, piece), piece), :]
     for d in range(1, n_col):
         total = total + part[d - 1]
     table[cell] = total
-    table_copies = [
-        remote(table.at[cell], table.at[cell], table_send.at[d - 1], table_recv.at[d - 1],
-               cell=lax.rem(cell + d, n_cell))
-        for d in range(1, n_cell)
-    ]
     for copy in table_copies:
         copy.start()
-
-    for q in range(CHUNKS):
-        near_arrive(q, 1)
-        near_start(q, 0)
-        near_arrive(q, 2)
-        near_start(q, 3)
+    for q in range(1, CHUNKS):
+        for p in (0, 3, 1, 2):
+            near_start(q, p)
+
+    def product(tile, buf, slot, q):
+        columns = pl.ds(pl.multiple_of(slot * rows + q * size, size), size)
+        acc[...] += across(buf[slot, q], tiles[tile, :, columns])
+
+    def pick(q):
+        picked = jnp.zeros(near.shape[2:], BF16)
+        for p, step in enumerate(OFFSETS):
+            near_arrive(q, p)
+            picked = jnp.where(use & (offset == step), near[p, q], picked)
+        beside[col, q] = picked
+        for d in order:
+            side_copies[d, q].start()
+
+    acc[...] = jnp.zeros_like(acc)
+    for name in ("count", "offset"):
+        loads[name].wait()
+    offset = offset_ref[cell]
+    use = count_ref[cell] == 2
     loads["tile0"].wait()
     for q in range(CHUNKS):
         product(0, own, col, q)
-    for h in order[1:]:
-        for q in range(CHUNKS):
-            arrive(own_copies, h, q)
-            begin(own_copies, h, q)
-        if h == bits[0]:
-            for q in range(CHUNKS):
-                product(0, own, flip(h), q)
-
-    for name in ("cores", "fsrc", "fcount", "count", "offset"):
+    for name in ("cores", "fsrc", "fcount"):
         loads[name].wait()
     rank = cores.shape[1]
     for k in range(0, cores.shape[0], 2):
         flat[:, k * rank:(k + 2) * rank] = jnp.concatenate([cores[k], cores[k + 1]], axis=1)
-
-    offset = offset_ref[cell]
-    use = count_ref[cell] == 2
-    for q in range(CHUNKS):
-        near_arrive(q, 0)
-        near_arrive(q, 3)
-        picked = jnp.zeros(near.shape[2:], BF16)
-        for p, step in enumerate(OFFSETS):
-            picked = jnp.where(use & (offset == step), near[p, q], picked)
-        beside[col, q] = picked
-        begin(side_copies, 0, q)
+    pick(0)
+    for q in range(CHUNKS):
+        for d in reversed(order):
+            own_copies[d, q].wait_recv()
+            if q == 0:
+                product(0, own, flip(d), q)
+    for q in range(1, CHUNKS):
+        pick(q)
 
     for copy in table_copies:
         copy.wait_recv()
@@ -217,23 +196,21 @@
     for copy in core_copies:
         copy.start()
 
-    for h in order[1:]:
-        if h != bits[0]:
-            for q in range(CHUNKS):
-                product(0, own, flip(h), q)
+    for q in range(1, CHUNKS):
+        for d in order:
+            product(0, own, flip(d), q)
     loads["tile1"].wait()
     for q in range(CHUNKS):
         product(1, beside, col, q)
-    for h in order[1:]:
-        for q in range(CHUNKS):
-            arrive(side_copies, h, q)
-            begin(side_copies, h, q)
-            product(1, beside, flip(h), q)
-
-    loads["bout"].wait()
-    for copy in core_copies:
-        copy.wait_recv()
-    out_ref[...] = acc[...] + jnp.dot(coret[...], bout[...], preferred_element_type=F32)
+    for q in range(CHUNKS):
+        if q == CHUNKS - 1:
+            loads["bout"].wait()
+            for copy in core_copies:
+                copy.wait_recv()
+            acc[...] += jnp.dot(coret[...], bout[...], preferred_element_type=F32)
+        for d in reversed(order):
+            side_copies[d, q].wait_recv()
+            product(1, beside, flip(d), q)
 
     for copy in part_copies + table_copies + core_copies:
         copy.wait_send()
@@ -276,7 +253,6 @@
             pltpu.VMEM((n_cell, piece, rank), F32),
             pltpu.VMEM((rank, far * rank), F32),
             pltpu.VMEM((width, rank), BF16),
-            pltpu.VMEM((width, rows), F32),
             dma(10),
             dma((n_col - 1) * CHUNKS), dma((n_col - 1) * CHUNKS),
             dma(len(OFFSETS) * CHUNKS), dma(len(OFFSETS) * CHUNKS),

time: 17.2 us -> 17 us (0.988); the launches traced: 16.9 us -> 16.9 us
  no operation moved by 1% of the time
where the time goes in v5:
time: 17 us; the launch traced here: 16.9 us
  Pallas kernels  16.2 us (95%)
  local copies, waits for them, and re-layouts  0.66 us (4%)
    pallas_call x1, Pallas kernels, body(): pl.pallas_call(functools.partial(kernel, n_cell, n_col), out_shape=pltpu....  16.2 us
    unnamed x1, local copies, waits for them, and re-layouts  0.66 us

profile of v5, /device:TPU:0, one launch (start us, length us, event | category | flops | bytes accessed | tf_op | source)
XLA Modules:
  0.0 16.9 jit_solution(16310866521829857579)
XLA Ops:
  0.0 16.2 %shard_map.91 = f32[64,512]{1,0:T(8,128)S(1)} custom-call(s32[4]{0:T(128)} %count_hbm.1, s32[4]{0:T(128)} %offset_hbm.1, s32[4,8]{1,0:T(4,128)} %fsrc_hbm.1, s32[4]{0:T(128)} %fcount_hbm.1, f32[64,512]{1,0:T(8,128)} %bitcast.5, bf16[1,2,512,2048]{3,2,1,0:T(8,128)(2,1)} %tiles_hbm.1, f32[1,8,64,64]{3,2,1,0:T(8,128)} %cores_hbm.1, bf16[64,512]{1,0:T(8,128)(2,1)} %bitcast.6, ...), custom_call_target="tpu_custom_call" | custom-call | tf_op jit(solution)/shard_map/pallas_call | solution.py:233
  16.2 0.7 %copy.11 = f32[512,64]{0,1:T(8,128)} copy(f32[512,64]{0,1:T(8,128)S(1)} %bitcast.4) | data formatting | bytes 262144

commit v6 on v5

--- a/solution.py
+++ b/solution.py
@@ -144,9 +144,12 @@
         for p in (0, 3, 1, 2):
             near_start(q, p)
 
-    def product(tile, buf, slot, q):
-        columns = pl.ds(pl.multiple_of(slot * rows + q * size, size), size)
-        acc[...] += across(buf[slot, q], tiles[tile, :, columns])
+    def product(tile, buf, chunks):
+        places = [(j, q) for j in range(n_col) for q in chunks]
+        blocks = jnp.concatenate([buf[j, q] for j, q in places], axis=1)
+        columns = jnp.concatenate(
+            [tiles[tile, :, j * rows + q * size:j * rows + (q + 1) * size] for j, q in places], axis=1)
+        return across(blocks, columns)
 
     def pick(q):
         picked = jnp.zeros(near.shape[2:], BF16)
@@ -157,25 +160,18 @@
         for d in order:
             side_copies[d, q].start()
 
-    acc[...] = jnp.zeros_like(acc)
-    for name in ("count", "offset"):
+    for name in ("count", "offset", "cores", "fsrc", "fcount"):
         loads[name].wait()
     offset = offset_ref[cell]
     use = count_ref[cell] == 2
-    loads["tile0"].wait()
-    for q in range(CHUNKS):
-        product(0, own, col, q)
-    for name in ("cores", "fsrc", "fcount"):
-        loads[name].wait()
     rank = cores.shape[1]
     for k in range(0, cores.shape[0], 2):
         flat[:, k * rank:(k + 2) * rank] = jnp.concatenate([cores[k], cores[k + 1]], axis=1)
     pick(0)
-    for q in range(CHUNKS):
-        for d in reversed(order):
-            own_copies[d, q].wait_recv()
-            if q == 0:
-                product(0, own, flip(d), q)
+    loads["tile0"].wait()
+    for copy in own_copies.values():
+        copy.wait_recv()
+    acc[...] = product(0, own, range(CHUNKS))
     for q in range(1, CHUNKS):
         pick(q)
 
@@ -196,21 +192,16 @@
     for copy in core_copies:
         copy.start()
 
-    for q in range(1, CHUNKS):
-        for d in order:
-            product(0, own, flip(d), q)
     loads["tile1"].wait()
-    for q in range(CHUNKS):
-        product(1, beside, col, q)
     for q in range(CHUNKS):
         if q == CHUNKS - 1:
             loads["bout"].wait()
             for copy in core_copies:
                 copy.wait_recv()
             acc[...] += jnp.dot(coret[...], bout[...], preferred_element_type=F32)
-        for d in reversed(order):
+        for d in order:
             side_copies[d, q].wait_recv()
-            product(1, beside, flip(d), q)
+        acc[...] += product(1, beside, [q])
 
     for copy in part_copies + table_copies + core_copies:
         copy.wait_send()

time: 17 us -> 17 us (level)
  no operation moved by 1% of the time
where the time goes in v6:
time: 17 us; the launch traced here: 16.9 us
  Pallas kernels  16.2 us (95%)
  local copies, waits for them, and re-layouts  0.66 us (4%)
    pallas_call x1, Pallas kernels, body(): pl.pallas_call(functools.partial(kernel, n_cell, n_col), out_shape=pltpu....  16.2 us
    unnamed x1, local copies, waits for them, and re-layouts  0.66 us

profile of v6, /device:TPU:0, one launch (start us, length us, event | category | flops | bytes accessed | tf_op | source)
XLA Modules:
  0.0 16.9 jit_solution(7457281326732560005)
XLA Ops:
  0.0 16.2 %shard_map.91 = f32[64,512]{1,0:T(8,128)S(1)} custom-call(s32[4]{0:T(128)} %count_hbm.1, s32[4]{0:T(128)} %offset_hbm.1, s32[4,8]{1,0:T(4,128)} %fsrc_hbm.1, s32[4]{0:T(128)} %fcount_hbm.1, f32[64,512]{1,0:T(8,128)} %bitcast.5, bf16[1,2,512,2048]{3,2,1,0:T(8,128)(2,1)} %tiles_hbm.1, f32[1,8,64,64]{3,2,1,0:T(8,128)} %cores_hbm.1, bf16[64,512]{1,0:T(8,128)(2,1)} %bitcast.6, ...), custom_call_target="tpu_custom_call" | custom-call | tf_op jit(solution)/shard_map/pallas_call | solution.py:224
  16.2 0.7 %copy.11 = f32[512,64]{0,1:T(8,128)} copy(f32[512,64]{0,1:T(8,128)S(1)} %bitcast.4) | data formatting | bytes 262144

commit v7 on v6

--- a/solution.py
+++ b/solution.py
@@ -30,15 +30,14 @@
     acc,
     count_ref, offset_ref, fsrc_ref, fcount_ref,
     grad, tiles, cores, bout, bin_,
-    own, near, beside, ppt, part, table, flat, coret,
+    own, near, beside, ppt, part, table, flat,
     local_sem, own_send, own_recv, near_send, near_recv, side_send, side_recv,
-    part_send, part_recv, table_send, table_recv, core_send, core_recv,
+    part_send, part_recv, table_send, table_recv,
 ):
     cell = lax.axis_index("cell")
     col = lax.axis_index("col")
     width, rows = grad.shape
     size = rows // CHUNKS
-    piece = width // n_col
     bits = [1 << b for b in reversed(range(n_col.bit_length() - 1))]
 
     def flip(d):
@@ -108,8 +107,7 @@
     own_copies = spread(own, own_send, own_recv)
     side_copies = spread(beside, side_send, side_recv)
     part_copies = [
-        remote(ppt.at[pl.ds(pl.multiple_of(flip(d) * piece, piece), piece)], part.at[d - 1],
-               part_send.at[d - 1], part_recv.at[d - 1], col=flip(d))
+        remote(ppt, part.at[d - 1], part_send.at[d - 1], part_recv.at[d - 1], col=flip(d))
         for d in range(1, n_col)
     ]
     table_copies = [
@@ -118,31 +116,31 @@
         for d in range(1, n_cell)
     ]
 
+    pl.semaphore_wait(barrier, (n_col - 1) + (n_cell - 1))
+
+    for p in (0, 3, 1, 2):
+        near_start(0, p)
     loads["bin"].wait()
     ppt[...] = across(rounded, bin_[...])
-    pl.semaphore_wait(barrier, (n_col - 1) + (n_cell - 1))
-
     for copy in part_copies:
         copy.start()
-    for p in (0, 3, 1, 2):
-        near_start(0, p)
     for q in range(CHUNKS):
         for d in order:
             own_copies[d, q].start()
+        if q + 1 < CHUNKS:
+            for p in (0, 3, 1, 2):
+                near_start(q + 1, p)
     for name in ("tile0", "cores", "fsrc", "fcount", "tile1", "bout"):
         loads[name].start()
 
     for copy in part_copies:
         copy.wait_recv()
-    total = ppt[pl.ds(pl.multiple_of(col * piece, piece), piece), :]
+    total = ppt[...]
     for d in range(1, n_col):
         total = total + part[d - 1]
     table[cell] = total
     for copy in table_copies:
         copy.start()
-    for q in range(1, CHUNKS):
-        for p in (0, 3, 1, 2):
-            near_start(q, p)
 
     def product(tile, buf, chunks):
         places = [(j, q) for j in range(n_col) for q in chunks]
@@ -182,28 +180,19 @@
     for k in range(cores.shape[0]):
         source = table[fsrc_ref[cell, k]]
         picks.append(jnp.where(k < used, source, jnp.zeros_like(source)))
-    mixed = across(jnp.concatenate(picks, axis=1), flat[...], precision=lax.Precision.HIGHEST)
-    mine = pl.ds(pl.multiple_of(col * piece, piece), piece)
-    coret[mine, :] = mixed.astype(BF16)
-    core_copies = [
-        remote(coret.at[mine], coret.at[mine], core_send.at[d - 1], core_recv.at[d - 1], col=flip(d))
-        for d in range(1, n_col)
-    ]
-    for copy in core_copies:
-        copy.start()
+    core = across(
+        jnp.concatenate(picks, axis=1), flat[...], precision=lax.Precision.HIGHEST).astype(BF16)
 
     loads["tile1"].wait()
     for q in range(CHUNKS):
         if q == CHUNKS - 1:
             loads["bout"].wait()
-            for copy in core_copies:
-                copy.wait_recv()
-            acc[...] += jnp.dot(coret[...], bout[...], preferred_element_type=F32)
+            acc[...] += jnp.dot(core, bout[...], preferred_element_type=F32)
         for d in order:
             side_copies[d, q].wait_recv()
         acc[...] += product(1, beside, [q])
 
-    for copy in part_copies + table_copies + core_copies:
+    for copy in part_copies + table_copies:
         copy.wait_send()
     for copy in list(own_copies.values()) + list(side_copies.values()):
         copy.wait_send()
@@ -218,7 +207,7 @@
     rows, width = grad.shape
     slots, _, clus = near_tiles.shape[1:]
     far, rank = far_cores.shape[1:3]
-    size, piece = rows // CHUNKS, width // n_col
+    size = rows // CHUNKS
     dma = lambda n: pltpu.SemaphoreType.DMA((max(n, 1),))
     hbm = pl.BlockSpec(memory_space=pltpu.HBM)
     out = pl.pallas_call(
@@ -240,17 +229,15 @@
             pltpu.VMEM((len(OFFSETS), CHUNKS, width, size), BF16),
             pltpu.VMEM((n_col, CHUNKS, width, size), BF16),
             pltpu.VMEM((width, rank), F32),
-            pltpu.VMEM((n_col - 1, piece, rank), F32),
-            pltpu.VMEM((n_cell, piece, rank), F32),
+            pltpu.VMEM((n_col - 1, width, rank), F32),
+            pltpu.VMEM((n_cell, width, rank), F32),
             pltpu.VMEM((rank, far * rank), F32),
-            pltpu.VMEM((width, rank), BF16),
             dma(10),
             dma((n_col - 1) * CHUNKS), dma((n_col - 1) * CHUNKS),
             dma(len(OFFSETS) * CHUNKS), dma(len(OFFSETS) * CHUNKS),
             dma((n_col - 1) * CHUNKS), dma((n_col - 1) * CHUNKS),
             dma(n_col - 1), dma(n_col - 1),
             dma(n_cell - 1), dma(n_cell - 1),
-            dma(n_col - 1), dma(n_col - 1),
         ],
         compiler_params=pltpu.CompilerParams(
             collective_id=0, has_side_effects=True, vmem_limit_bytes=56 * 1024 * 1024

time: 17 us -> 16.5 us (0.971)
  Pallas kernels: 16.2 us -> 15.7 us
    pallas_call x1, Pallas kernels: 16.2 us -> 15.7 us  [body(): pl.pallas_call(functools.partial(kernel, n_cell, n_col), out_shape=pltpu....]
where the time goes in v7:
time: 16.5 us; the launch traced here: 16.4 us
  Pallas kernels  15.7 us (95%)
  local copies, waits for them, and re-layouts  0.66 us (4%)
    pallas_call x1, Pallas kernels, body(): pl.pallas_call(functools.partial(kernel, n_cell, n_col), out_shape=pltpu....  15.7 us
    unnamed x1, local copies, waits for them, and re-layouts  0.66 us

profile of v7, /device:TPU:0, one launch (start us, length us, event | category | flops | bytes accessed | tf_op | source)
XLA Modules:
  0.0 16.4 jit_solution(17814853132168150351)
XLA Ops:
  0.0 15.7 %shard_map.91 = f32[64,512]{1,0:T(8,128)S(1)} custom-call(s32[4]{0:T(128)} %count_hbm.1, s32[4]{0:T(128)} %offset_hbm.1, s32[4,8]{1,0:T(4,128)} %fsrc_hbm.1, s32[4]{0:T(128)} %fcount_hbm.1, f32[64,512]{1,0:T(8,128)} %bitcast.5, bf16[1,2,512,2048]{3,2,1,0:T(8,128)(2,1)} %tiles_hbm.1, f32[1,8,64,64]{3,2,1,0:T(8,128)} %cores_hbm.1, bf16[64,512]{1,0:T(8,128)(2,1)} %bitcast.6, ...), custom_call_target="tpu_custom_call" | custom-call | tf_op jit(solution)/shard_map/pallas_call | solution.py:213
  15.7 0.7 %copy.11 = f32[512,64]{0,1:T(8,128)} copy(f32[512,64]{0,1:T(8,128)S(1)} %bitcast.4) | data formatting | bytes 262144

commit v8 on v7

--- a/solution.py
+++ b/solution.py
@@ -9,7 +9,7 @@
 
 MESH = pl.DeviceIdType.MESH
 OFFSETS = (-2, -1, 1, 2)
-CHUNKS = 2
+CHUNKS = 4
 F32 = jnp.float32
 BF16 = jnp.bfloat16
 
@@ -104,7 +104,14 @@
             for d in range(1, n_col) for q in range(CHUNKS)
         }
 
-    own_copies = spread(own, own_send, own_recv)
+    own_copies, held = {}, [0]
+    for b in bits:
+        for h in held:
+            slot, index = flip(h), len(own_copies)
+            own_copies[h, b] = remote(
+                own.at[slot], own.at[slot], own_send.at[index], own_recv.at[index], col=flip(b))
+        held = held + [h ^ b for h in held]
+
     side_copies = spread(beside, side_send, side_recv)
     part_copies = [
         remote(ppt, part.at[d - 1], part_send.at[d - 1], part_recv.at[d - 1], col=flip(d))
@@ -124,12 +131,12 @@
     ppt[...] = across(rounded, bin_[...])
     for copy in part_copies:
         copy.start()
-    for q in range(CHUNKS):
-        for d in order:
-            own_copies[d, q].start()
-        if q + 1 < CHUNKS:
-            for p in (0, 3, 1, 2):
-                near_start(q + 1, p)
+    for q in range(1, CHUNKS):
+        for p in (0, 3, 1, 2):
+            near_start(q, p)
+        if q == 1:
+            for b in bits:
+                own_copies[0, b].start()
     for name in ("tile0", "cores", "fsrc", "fcount", "tile1", "bout"):
         loads[name].start()
 
@@ -166,12 +173,18 @@
     for k in range(0, cores.shape[0], 2):
         flat[:, k * rank:(k + 2) * rank] = jnp.concatenate([cores[k], cores[k + 1]], axis=1)
     pick(0)
+    for h in held[1:]:
+        for (source, b), copy in own_copies.items():
+            if source ^ b == h:
+                copy.wait_recv()
+        for (source, b), copy in own_copies.items():
+            if source == h:
+                copy.start()
+        if h == bits[0]:
+            for q in range(1, CHUNKS):
+                pick(q)
     loads["tile0"].wait()
-    for copy in own_copies.values():
-        copy.wait_recv()
     acc[...] = product(0, own, range(CHUNKS))
-    for q in range(1, CHUNKS):
-        pick(q)
 
     for copy in table_copies:
         copy.wait_recv()
@@ -184,13 +197,15 @@
         jnp.concatenate(picks, axis=1), flat[...], precision=lax.Precision.HIGHEST).astype(BF16)
 
     loads["tile1"].wait()
-    for q in range(CHUNKS):
-        if q == CHUNKS - 1:
-            loads["bout"].wait()
-            acc[...] += jnp.dot(core, bout[...], preferred_element_type=F32)
-        for d in order:
+    for d in order:
+        for q in range(CHUNKS - 1):
             side_copies[d, q].wait_recv()
-        acc[...] += product(1, beside, [q])
+    acc[...] += product(1, beside, range(CHUNKS - 1))
+    loads["bout"].wait()
+    acc[...] += jnp.dot(core, bout[...], preferred_element_type=F32)
+    for d in order:
+        side_copies[d, CHUNKS - 1].wait_recv()
+    acc[...] += product(1, beside, [CHUNKS - 1])
 
     for copy in part_copies + table_copies:
         copy.wait_send()
@@ -233,7 +248,7 @@
             pltpu.VMEM((n_cell, width, rank), F32),
             pltpu.VMEM((rank, far * rank), F32),
             dma(10),
-            dma((n_col - 1) * CHUNKS), dma((n_col - 1) * CHUNKS),
+            dma(n_col - 1), dma(n_col - 1),
             dma(len(OFFSETS) * CHUNKS), dma(len(OFFSETS) * CHUNKS),
             dma((n_col - 1) * CHUNKS), dma((n_col - 1) * CHUNKS),
             dma(n_col - 1), dma(n_col - 1),

time: 16.5 us -> 15.9 us (0.964)
  Pallas kernels: 15.7 us -> 15.1 us
    pallas_call x1, Pallas kernels: 15.7 us -> 15.1 us  [body(): pl.pallas_call(functools.partial(kernel, n_cell, n_col), out_shape=pltpu....]
where the time goes in v8:
time: 15.9 us; the launch traced here: 15.8 us
  Pallas kernels  15.1 us (95%)
  local copies, waits for them, and re-layouts  0.66 us (4%)
    pallas_call x1, Pallas kernels, body(): pl.pallas_call(functools.partial(kernel, n_cell, n_col), out_shape=pltpu....  15.1 us
    unnamed x1, local copies, waits for them, and re-layouts  0.66 us

profile of v8, /device:TPU:0, one launch (start us, length us, event | category | flops | bytes accessed | tf_op | source)
XLA Modules:
  0.0 15.8 jit_solution(7911993800295838517)
XLA Ops:
  0.0 15.1 %shard_map.91 = f32[64,512]{1,0:T(8,128)S(1)} custom-call(s32[4]{0:T(128)} %count_hbm.1, s32[4]{0:T(128)} %offset_hbm.1, s32[4,8]{1,0:T(4,128)} %fsrc_hbm.1, s32[4]{0:T(128)} %fcount_hbm.1, f32[64,512]{1,0:T(8,128)} %bitcast.5, bf16[1,2,512,2048]{3,2,1,0:T(8,128)(2,1)} %tiles_hbm.1, f32[1,8,64,64]{3,2,1,0:T(8,128)} %cores_hbm.1, bf16[64,512]{1,0:T(8,128)(2,1)} %bitcast.6, ...), custom_call_target="tpu_custom_call" | custom-call | tf_op jit(solution)/shard_map/pallas_call | solution.py:228
  15.1 0.7 %copy.11 = f32[512,64]{0,1:T(8,128)} copy(f32[512,64]{0,1:T(8,128)S(1)} %bitcast.4) | data formatting | bytes 262144

commit v9 on v7

--- a/solution.py
+++ b/solution.py
@@ -9,7 +9,8 @@
 
 MESH = pl.DeviceIdType.MESH
 OFFSETS = (-2, -1, 1, 2)
-CHUNKS = 2
+CHUNKS = 4
+FORWARDED = 2
 F32 = jnp.float32
 BF16 = jnp.bfloat16
 
@@ -78,14 +79,19 @@
     for q in range(CHUNKS):
         own[col, q] = rounded[:, q * size:(q + 1) * size]
 
+    up, down = jnp.minimum(cell + 1, n_cell - 1), jnp.maximum(cell - 1, 0)
+    below, above = cell > 0, cell < n_cell - 1
+    inner = below & above
     near_copies, near_when = {}, {}
     for q in range(CHUNKS):
-        for p, step in enumerate(OFFSETS):
+        for p, src, target, when in (
+            (0, near.at[1, q], up, inner), (1, own.at[col, q], up, above),
+            (2, own.at[col, q], down, below), (3, near.at[2, q], down, inner),
+        ):
             index = q * len(OFFSETS) + p
             near_copies[q, p] = remote(
-                own.at[col, q], near.at[p, q], near_send.at[index], near_recv.at[index],
-                cell=jnp.clip(cell - step, 0, n_cell - 1))
-            near_when[p] = (cell - step >= 0) & (cell - step < n_cell)
+                src, near.at[p, q], near_send.at[index], near_recv.at[index], cell=target)
+            near_when[p] = when
 
     def near_start(q, p):
         pl.when(near_when[p])(near_copies[q, p].start)
@@ -95,17 +101,41 @@
         pl.when((cell + step >= 0) & (cell + step < n_cell))(near_copies[q, p].wait_recv)
 
     order = list(range(2, n_col)) + [1]
-
-    def spread(buf, send, recv):
+    held = [0]
+    for b in bits:
+        held += [h ^ b for h in held]
+
+    def cube(view, send, recv, first):
+        copies, here = {}, [0]
+        for b in bits:
+            for h in here:
+                slot, index = flip(h), first + len(copies)
+                copies[h, b] = remote(view(slot), view(slot), send.at[index], recv.at[index], col=flip(b))
+            here = here + [h ^ b for h in here]
+        return copies
+
+    def spread(view, send, recv, first):
         return {
-            (d, q): remote(
-                buf.at[col, q], buf.at[col, q], send.at[(d - 1) * CHUNKS + q],
-                recv.at[(d - 1) * CHUNKS + q], col=flip(d))
-            for d in range(1, n_col) for q in range(CHUNKS)
+            (0, d): remote(view(col), view(col), send.at[first + i], recv.at[first + i], col=flip(d))
+            for i, d in enumerate(order)
         }
 
-    own_copies = spread(own, own_send, own_recv)
-    side_copies = spread(beside, side_send, side_recv)
+    def start(copies, h):
+        for (source, b), copy in copies.items():
+            if source == h:
+                copy.start()
+
+    def arrive(copies, h):
+        for (source, b), copy in copies.items():
+            if source ^ b == h:
+                copy.wait_recv()
+
+    own_copies = cube(lambda slot: own.at[slot], own_send, own_recv, 0)
+    side_copies = [
+        (cube if q < FORWARDED else spread)(
+            lambda slot, q=q: beside.at[slot, q], side_send, side_recv, q * (n_col - 1))
+        for q in range(CHUNKS)
+    ]
     part_copies = [
         remote(ppt, part.at[d - 1], part_send.at[d - 1], part_recv.at[d - 1], col=flip(d))
         for d in range(1, n_col)
@@ -118,20 +148,23 @@
 
     pl.semaphore_wait(barrier, (n_col - 1) + (n_cell - 1))
 
-    for p in (0, 3, 1, 2):
-        near_start(0, p)
+    near_start(0, 1)
+    near_start(0, 2)
     loads["bin"].wait()
     ppt[...] = across(rounded, bin_[...])
     for copy in part_copies:
         copy.start()
-    for q in range(CHUNKS):
-        for d in order:
-            own_copies[d, q].start()
-        if q + 1 < CHUNKS:
-            for p in (0, 3, 1, 2):
-                near_start(q + 1, p)
+    for q in range(1, CHUNKS):
+        near_start(q, 1)
+        near_start(q, 2)
+    start(own_copies, 0)
     for name in ("tile0", "cores", "fsrc", "fcount", "tile1", "bout"):
         loads[name].start()
+    for q in range(CHUNKS):
+        near_arrive(q, 1)
+        near_start(q, 0)
+        near_arrive(q, 2)
+        near_start(q, 3)
 
     for copy in part_copies:
         copy.wait_recv()
@@ -150,13 +183,13 @@
         return across(blocks, columns)
 
     def pick(q):
+        near_arrive(q, 0)
+        near_arrive(q, 3)
         picked = jnp.zeros(near.shape[2:], BF16)
         for p, step in enumerate(OFFSETS):
-            near_arrive(q, p)
             picked = jnp.where(use & (offset == step), near[p, q], picked)
         beside[col, q] = picked
-        for d in order:
-            side_copies[d, q].start()
+        start(side_copies[q], 0)
 
     for name in ("count", "offset", "cores", "fsrc", "fcount"):
         loads[name].wait()
@@ -165,13 +198,19 @@
     rank = cores.shape[1]
     for k in range(0, cores.shape[0], 2):
         flat[:, k * rank:(k + 2) * rank] = jnp.concatenate([cores[k], cores[k + 1]], axis=1)
-    pick(0)
+    arrive(own_copies, bits[0])
+    start(own_copies, bits[0])
+    for q in range(CHUNKS):
+        pick(q)
+    for h in held[2:]:
+        arrive(own_copies, h)
+        start(own_copies, h)
     loads["tile0"].wait()
-    for copy in own_copies.values():
-        copy.wait_recv()
     acc[...] = product(0, own, range(CHUNKS))
-    for q in range(1, CHUNKS):
-        pick(q)
+    for h in held[1:-1]:
+        for q in range(FORWARDED):
+            arrive(side_copies[q], h)
+            start(side_copies[q], h)
 
     for copy in table_copies:
         copy.wait_recv()
@@ -184,18 +223,21 @@
         jnp.concatenate(picks, axis=1), flat[...], precision=lax.Precision.HIGHEST).astype(BF16)
 
     loads["tile1"].wait()
-    for q in range(CHUNKS):
-        if q == CHUNKS - 1:
-            loads["bout"].wait()
+    loads["bout"].wait()
+    for turn in range(2):
+        chunks = list(range(turn, CHUNKS, 2))
+        for q in chunks:
+            for h in held[-1:] if q < FORWARDED else held[1:]:
+                arrive(side_copies[q], h)
+        acc[...] += product(1, beside, chunks)
+        if turn == 0:
             acc[...] += jnp.dot(core, bout[...], preferred_element_type=F32)
-        for d in order:
-            side_copies[d, q].wait_recv()
-        acc[...] += product(1, beside, [q])
 
     for copy in part_copies + table_copies:
         copy.wait_send()
-    for copy in list(own_copies.values()) + list(side_copies.values()):
-        copy.wait_send()
+    for copies in [own_copies] + side_copies:
+        for copy in copies.values():
+            copy.wait_send()
     for (_, p), copy in near_copies.items():
         pl.when(near_when[p])(copy.wait_send)
 
@@ -233,7 +275,7 @@
             pltpu.VMEM((n_cell, width, rank), F32),
             pltpu.VMEM((rank, far * rank), F32),
             dma(10),
-            dma((n_col - 1) * CHUNKS), dma((n_col - 1) * CHUNKS),
+            dma(n_col - 1), dma(n_col - 1),
             dma(len(OFFSETS) * CHUNKS), dma(len(OFFSETS) * CHUNKS),
             dma((n_col - 1) * CHUNKS), dma((n_col - 1) * CHUNKS),
             dma(n_col - 1), dma(n_col - 1),

time: 16.5 us -> 17.4 us (1.055)
  Pallas kernels: 15.7 us -> 16.6 us
    pallas_call x1, Pallas kernels: 15.7 us -> 16.6 us  [body(): pl.pallas_call(functools.partial(kernel, n_cell, n_col), out_shape=pltpu....]
where the time goes in v9:
time: 17.4 us; the launch traced here: 17.2 us
  Pallas kernels  16.6 us (95%)
  local copies, waits for them, and re-layouts  0.66 us (4%)
    pallas_call x1, Pallas kernels, body(): pl.pallas_call(functools.partial(kernel, n_cell, n_col), out_shape=pltpu....  16.6 us
    unnamed x1, local copies, waits for them, and re-layouts  0.66 us

profile of v9, /device:TPU:0, one launch (start us, length us, event | category | flops | bytes accessed | tf_op | source)
XLA Modules:
  0.0 17.2 jit_solution(12404850488229978129)
XLA Ops:
  0.0 16.6 %shard_map.91 = f32[64,512]{1,0:T(8,128)S(1)} custom-call(s32[4]{0:T(128)} %count_hbm.1, s32[4]{0:T(128)} %offset_hbm.1, s32[4,8]{1,0:T(4,128)} %fsrc_hbm.1, s32[4]{0:T(128)} %fcount_hbm.1, f32[64,512]{1,0:T(8,128)} %bitcast.5, bf16[1,2,512,2048]{3,2,1,0:T(8,128)(2,1)} %tiles_hbm.1, f32[1,8,64,64]{3,2,1,0:T(8,128)} %cores_hbm.1, bf16[64,512]{1,0:T(8,128)(2,1)} %bitcast.6, ...), custom_call_target="tpu_custom_call" | custom-call | tf_op jit(solution)/shard_map/pallas_call | solution.py:255
  16.6 0.7 %copy.11 = f32[512,64]{0,1:T(8,128)} copy(f32[512,64]{0,1:T(8,128)S(1)} %bitcast.4) | data formatting | bytes 262144

commit v10 on v8

--- a/solution.py
+++ b/solution.py
@@ -66,7 +66,7 @@
         name: pltpu.make_async_copy(src, dst, local_sem.at[i])
         for i, (name, (src, dst)) in enumerate(pairs.items())
     }
-    for name in ("grad", "bin", "count", "offset"):
+    for name in ("grad", "bin", "count", "offset", "fsrc", "fcount", "cores", "tile0", "tile1", "bout"):
         loads[name].start()
 
     for p, step in enumerate(OFFSETS):
@@ -137,8 +137,6 @@
         if q == 1:
             for b in bits:
                 own_copies[0, b].start()
-    for name in ("tile0", "cores", "fsrc", "fcount", "tile1", "bout"):
-        loads[name].start()
 
     for copy in part_copies:
         copy.wait_recv()
@@ -186,6 +184,14 @@
     loads["tile0"].wait()
     acc[...] = product(0, own, range(CHUNKS))
 
+    def beside_term(chunks):
+        for q in chunks:
+            for d in order:
+                side_copies[d, q].wait_recv()
+        acc[...] += product(1, beside, chunks)
+
+    loads["tile1"].wait()
+    beside_term(range(CHUNKS // 2))
     for copy in table_copies:
         copy.wait_recv()
     used = fcount_ref[cell]
@@ -196,16 +202,10 @@
     core = across(
         jnp.concatenate(picks, axis=1), flat[...], precision=lax.Precision.HIGHEST).astype(BF16)
 
-    loads["tile1"].wait()
-    for d in order:
-        for q in range(CHUNKS - 1):
-            side_copies[d, q].wait_recv()
-    acc[...] += product(1, beside, range(CHUNKS - 1))
     loads["bout"].wait()
     acc[...] += jnp.dot(core, bout[...], preferred_element_type=F32)
-    for d in order:
-        side_copies[d, CHUNKS - 1].wait_recv()
-    acc[...] += product(1, beside, [CHUNKS - 1])
+    for q in range(CHUNKS // 2, CHUNKS):
+        beside_term([q])
 
     for copy in part_copies + table_copies:
         copy.wait_send()

time: 15.9 us -> 15.6 us (0.981)
  Pallas kernels: 15.1 us -> 14.8 us
    pallas_call x1, Pallas kernels: 15.1 us -> 14.8 us  [body(): pl.pallas_call(functools.partial(kernel, n_cell, n_col), out_shape=pltpu....]
where the time goes in v10:
time: 15.6 us; the launch traced here: 15.4 us
  Pallas kernels  14.8 us (95%)
  local copies, waits for them, and re-layouts  0.66 us (4%)
    pallas_call x1, Pallas kernels, body(): pl.pallas_call(functools.partial(kernel, n_cell, n_col), out_shape=pltpu....  14.8 us
    unnamed x1, local copies, waits for them, and re-layouts  0.66 us

profile of v10, /device:TPU:0, one launch (start us, length us, event | category | flops | bytes accessed | tf_op | source)
XLA Modules:
  0.0 15.4 jit_solution(2621048799515614479)
XLA Ops:
  0.0 14.8 %shard_map.91 = f32[64,512]{1,0:T(8,128)S(1)} custom-call(s32[4]{0:T(128)} %count_hbm.1, s32[4]{0:T(128)} %offset_hbm.1, s32[4,8]{1,0:T(4,128)} %fsrc_hbm.1, s32[4]{0:T(128)} %fcount_hbm.1, f32[64,512]{1,0:T(8,128)} %bitcast.5, bf16[1,2,512,2048]{3,2,1,0:T(8,128)(2,1)} %tiles_hbm.1, f32[1,8,64,64]{3,2,1,0:T(8,128)} %cores_hbm.1, bf16[64,512]{1,0:T(8,128)(2,1)} %bitcast.6, ...), custom_call_target="tpu_custom_call" | custom-call | tf_op jit(solution)/shard_map/pallas_call | solution.py:228
  14.8 0.7 %copy.11 = f32[512,64]{0,1:T(8,128)} copy(f32[512,64]{0,1:T(8,128)S(1)} %bitcast.4) | data formatting | bytes 262144

commit v11 on v10

--- a/solution.py
+++ b/solution.py
@@ -170,7 +170,8 @@
     rank = cores.shape[1]
     for k in range(0, cores.shape[0], 2):
         flat[:, k * rank:(k + 2) * rank] = jnp.concatenate([cores[k], cores[k + 1]], axis=1)
-    pick(0)
+    for q in range(CHUNKS // 2):
+        pick(q)
     for h in held[1:]:
         for (source, b), copy in own_copies.items():
             if source ^ b == h:
@@ -179,7 +180,7 @@
             if source == h:
                 copy.start()
         if h == bits[0]:
-            for q in range(1, CHUNKS):
+            for q in range(CHUNKS // 2, CHUNKS):
                 pick(q)
     loads["tile0"].wait()
     acc[...] = product(0, own, range(CHUNKS))

time: 15.6 us -> 15.6 us (level)
  no operation moved by 1% of the time
where the time goes in v11:
time: 15.6 us; the launch traced here: 15.4 us
  Pallas kernels  14.8 us (95%)
  local copies, waits for them, and re-layouts  0.66 us (4%)
    pallas_call x1, Pallas kernels, body(): pl.pallas_call(functools.partial(kernel, n_cell, n_col), out_shape=pltpu....  14.8 us
    unnamed x1, local copies, waits for them, and re-layouts  0.66 us

profile of v11, /device:TPU:0, one launch (start us, length us, event | category | flops | bytes accessed | tf_op | source)
XLA Modules:
  0.0 15.4 jit_solution(17357963909478062650)
XLA Ops:
  0.0 14.8 %shard_map.91 = f32[64,512]{1,0:T(8,128)S(1)} custom-call(s32[4]{0:T(128)} %count_hbm.1, s32[4]{0:T(128)} %offset_hbm.1, s32[4,8]{1,0:T(4,128)} %fsrc_hbm.1, s32[4]{0:T(128)} %fcount_hbm.1, f32[64,512]{1,0:T(8,128)} %bitcast.5, bf16[1,2,512,2048]{3,2,1,0:T(8,128)(2,1)} %tiles_hbm.1, f32[1,8,64,64]{3,2,1,0:T(8,128)} %cores_hbm.1, bf16[64,512]{1,0:T(8,128)(2,1)} %bitcast.6, ...), custom_call_target="tpu_custom_call" | custom-call | tf_op jit(solution)/shard_map/pallas_call | solution.py:229
  14.8 0.7 %copy.11 = f32[512,64]{0,1:T(8,128)} copy(f32[512,64]{0,1:T(8,128)S(1)} %bitcast.4) | data formatting | bytes 262144

commit v12 on v11

--- a/solution.py
+++ b/solution.py
@@ -134,7 +134,7 @@
     for q in range(1, CHUNKS):
         for p in (0, 3, 1, 2):
             near_start(q, p)
-        if q == 1:
+        if q == CHUNKS - 1:
             for b in bits:
                 own_copies[0, b].start()
 

time: 15.6 us -> 15.6 us (level)
  no operation moved by 1% of the time
where the time goes in v12:
time: 15.6 us; the launch traced here: 15.4 us
  Pallas kernels  14.8 us (95%)
  local copies, waits for them, and re-layouts  0.66 us (4%)
    pallas_call x1, Pallas kernels, body(): pl.pallas_call(functools.partial(kernel, n_cell, n_col), out_shape=pltpu....  14.8 us
    unnamed x1, local copies, waits for them, and re-layouts  0.66 us

profile of v12, /device:TPU:0, one launch (start us, length us, event | category | flops | bytes accessed | tf_op | source)
XLA Modules:
  0.0 15.4 jit_solution(8869033865891303812)
XLA Ops:
  0.0 14.8 %shard_map.91 = f32[64,512]{1,0:T(8,128)S(1)} custom-call(s32[4]{0:T(128)} %count_hbm.1, s32[4]{0:T(128)} %offset_hbm.1, s32[4,8]{1,0:T(4,128)} %fsrc_hbm.1, s32[4]{0:T(128)} %fcount_hbm.1, f32[64,512]{1,0:T(8,128)} %bitcast.5, bf16[1,2,512,2048]{3,2,1,0:T(8,128)(2,1)} %tiles_hbm.1, f32[1,8,64,64]{3,2,1,0:T(8,128)} %cores_hbm.1, bf16[64,512]{1,0:T(8,128)(2,1)} %bitcast.6, ...), custom_call_target="tpu_custom_call" | custom-call | tf_op jit(solution)/shard_map/pallas_call | solution.py:229
  14.8 0.7 %copy.11 = f32[512,64]{0,1:T(8,128)} copy(f32[512,64]{0,1:T(8,128)S(1)} %bitcast.4) | data formatting | bytes 262144
